TPU v7x, 32 devices: a whole 2x2x4 slice. The times are simulated.
32 devices in a mesh: ctx: 8 (over z, y), fsdp: 4 (over x, core).
Axes of the slice: x: 2, y: 2, z: 4, core: 2. Of those that a mesh axis runs over, the one named last changes fastest.
Arguments:
- inputs: float32 [4, 2, 1024, 1024], P('fsdp', None, 'ctx'), may hold values from -6 to 6
- cotangent: float32 [4, 2, 1024, 1024], P('fsdp', None, 'ctx'), may hold values from -6 to 6
- doc_lengths: int32 [4, 4], P('fsdp'), may hold values from 4 to 1536, as said below
- routes: int32 [4, 2, 1024, 8], P('fsdp', None, 'ctx'), may hold values from 0 to 31, all different within a row
- attn_gain: bfloat16 [1024], P('fsdp'), may hold values from 0.5 to 1.5
- ffn_gain: bfloat16 [1024], P('fsdp'), may hold values from 0.5 to 1.5
- w_query: bfloat16 [1024, 1024], P('fsdp'), may hold values from -0.75 to 0.75
- key_weight: bfloat16 [1024, 512], P('fsdp'), may hold values from -0.75 to 0.75
- value_weight: bfloat16 [1024, 512], P('fsdp'), may hold values from -0.1875 to 0.1875
- w_out: bfloat16 [1024, 1024], P('fsdp'), may hold values from -12 to 12
- w_router: bfloat16 [1024, 32], P('fsdp'), may hold values from -0.095703125 to 0.095703125
- w_gate: bfloat16 [32, 1024, 512], P('fsdp'), may hold values from -0.1875 to 0.1875
- w_up: bfloat16 [32, 1024, 512], P('fsdp'), may hold values from -0.1875 to 0.1875
- w_down: bfloat16 [32, 512, 1024], P('fsdp'), may hold values from -21 to 21
Outputs:
- mixed: float32 [4, 2, 1024, 1024], P('fsdp', None, 'ctx')
- grad_inputs: float32 [4, 2, 1024, 1024], P('fsdp', None, 'ctx')
- grad_attn_gain: float32 [1024], P('fsdp')
- grad_ffn_gain: float32 [1024], P('fsdp')
- grad_w_query: float32 [1024, 1024], P('fsdp')
- grad_w_key: float32 [1024, 512], P('fsdp')
- grad_w_value: float32 [1024, 512], P('fsdp')
- grad_w_out: float32 [1024, 1024], P('fsdp')
- grad_w_router: float32 [1024, 32], P('fsdp')
- grad_w_gate: float32 [32, 1024, 512], P('fsdp')
- grad_w_up: float32 [32, 1024, 512], P('fsdp')
- grad_w_down: float32 [32, 512, 1024], P('fsdp')
Inputs may be any that keep to these rules, and one draw needn't show every extreme that they name: `doc_lengths`: each row's lengths sum to 2048; the first document of every sequence covers at least its first half. `routes`: each token names 8 different experts.
All inputs are finite; a program needn't handle non-finite values.
Results may differ from a plain program's by a relative error of at most 0.024.
Values may be sent and summed in bfloat16 or wider, within the bound.
A program may use at most 576 MiB of HBM per device.

v0:
```python
import functools

import jax
import jax.numpy as jnp
import numpy as np
from jax import lax
from jax.experimental import pallas as pl
from jax.experimental.pallas import tpu as pltpu
from jax.sharding import PartitionSpec as P

QUERY_HEADS = 16
KEY_VALUE_HEADS = 8
HEAD_DIMENSION = 64
EXPERTS = 32
TOP = 8

ATTN_SCALE = 0.015625
RESIDUAL = 0.22
NORM_EPS = 1e-06
ROPE_BASE = 10000.0
MASKED = -1e30

F32 = jnp.float32
BF16 = jnp.bfloat16
MIB = 1 << 20
NT = (((1,), (1,)), ((), ()))
TN = (((0,), (0,)), ((), ()))
BLK = 256
PACK = 256


def dot(a, b, dims=None):
    if dims is None:
        return jnp.dot(a, b, preferred_element_type=F32)
    return lax.dot_general(a, b, dims, preferred_element_type=F32)


def params(limit=56, **kw):
    return pltpu.CompilerParams(vmem_limit_bytes=limit * MIB, **kw)


def cost(flops, bytes_accessed):
    return pl.CostEstimate(flops=int(flops), bytes_accessed=int(bytes_accessed), transcendentals=0)


def lane_iota(shape):
    return lax.broadcasted_iota(jnp.int32, shape, len(shape) - 1)


def row_iota(shape):
    return lax.broadcasted_iota(jnp.int32, shape, len(shape) - 2)


def rotary_table(length):
    half = length // 2
    order = np.arange(half, dtype=np.float32)
    positions = np.concatenate([order, length - 1 - order]).astype(np.float32)
    m = np.arange(HEAD_DIMENSION // 2, dtype=np.float64)
    frequency = (ROPE_BASE ** (-2.0 * m / HEAD_DIMENSION)).astype(np.float32)
    angles = (positions[:, None] * frequency[None, :]).astype(np.float64)
    cosine, sine = np.cos(angles), np.sin(angles)
    cos_head = np.concatenate([cosine, cosine], -1)
    sin_head = np.concatenate([-sine, sine], -1)
    return np.concatenate([cos_head, cos_head, sin_head, sin_head], -1).astype(np.float32)


def turn(v, table, direction):
    lanes = lane_iota(v.shape)
    cosine = jnp.concatenate([table[:, :128], table[:, :128]], -1)
    sine = jnp.concatenate([table[:, 128:], table[:, 128:]], -1)
    turned = lanes < 3 * HEAD_DIMENSION
    swapped = jnp.where(lanes % HEAD_DIMENSION < HEAD_DIMENSION // 2, pltpu.roll(v, PACK - 32, 1), pltpu.roll(v, 32, 1))
    return jnp.where(turned, v * cosine + direction * (swapped * sine), v)


def norm_parts(values):
    inv_rms = lax.rsqrt(jnp.mean(values * values, -1, keepdims=True) + NORM_EPS)
    return values * inv_rms, inv_rms


def norm_back(grad_normed, normed, inv_rms):
    return inv_rms * (grad_normed - normed * jnp.mean(grad_normed * normed, -1, keepdims=True))


def prep_kernel(cap, routes_ref, cot_ref, out_ref):
    tokens, width = cot_ref.shape
    earlier = (row_iota((tokens, tokens)) < lane_iota((tokens, tokens))).astype(BF16)
    experts = row_iota((EXPERTS, tokens))
    base = jnp.zeros((EXPERTS, 1), F32)
    plus = jnp.zeros((EXPERTS, tokens), F32)
    for k in range(TOP):
        row = jnp.concatenate([routes_ref[0, k : k + 1, :], routes_ref[1, k : k + 1, :]], 1)
        chosen = experts == row
        ones = chosen.astype(F32)
        slot = dot(ones.astype(BF16), earlier) + base
        plus = plus + jnp.where(chosen & (slot < cap), slot + 1.0, 0.0)
        base = base + jnp.sum(ones, 1, keepdims=True)
    out_ref[:tokens, :] = cot_ref[...].astype(BF16)
    out_ref[tokens:, :] = jnp.concatenate([plus - 1.0, jnp.zeros((EXPERTS, width - tokens), F32)], -1).astype(BF16)


def prep(routes, cot, cap):
    tokens, width = cot.shape
    return pl.pallas_call(
        functools.partial(prep_kernel, cap),
        out_shape=jax.ShapeDtypeStruct((tokens + EXPERTS, width), BF16),
        compiler_params=params(),
        cost_estimate=cost(1e9, 2e6),
        name="prep",
    )(routes, cot)


def qkv_kernel(shard, x_ref, gain_ref, w_ref, table_ref, out_ref, h_ref):
    @pl.when(pl.program_id(0) == 0)
    def _():
        normed, _ = norm_parts(x_ref[...])
        h_ref[...] = (normed * gain_ref[...]).astype(BF16)

    total = None
    for f in range(w_ref.shape[0]):
        part = dot(h_ref[:, f * shard : (f + 1) * shard], w_ref[f, :shard, :])
        total = part if total is None else total + part
    for d in range(out_ref.shape[0]):
        out_ref[d] = turn(total[:, d * PACK : (d + 1) * PACK], table_ref[...], 1.0).astype(BF16)


def qkv(x, gain, weights, table, shard, n):
    tokens, width = x.shape
    fsdp, padded, _ = weights.shape
    return pl.pallas_call(
        functools.partial(qkv_kernel, shard),
        grid=(n // 2,),
        in_specs=[
            pl.BlockSpec((tokens, width), lambda i: (0, 0)),
            pl.BlockSpec((1, width), lambda i: (0, 0)),
            pl.BlockSpec((fsdp, padded, 2 * PACK), lambda i: (0, 0, i)),
            pl.BlockSpec((tokens, 256), lambda i: (0, 0)),
        ],
        out_specs=[
            pl.BlockSpec((2, tokens, PACK), lambda i: (i, 0, 0)),
            pl.BlockSpec((tokens, width), lambda i: (0, 0)),
        ],
        out_shape=[
            jax.ShapeDtypeStruct((n, tokens, PACK), BF16),
            jax.ShapeDtypeStruct((tokens, width), BF16),
        ],
        compiler_params=params(),
        cost_estimate=cost(2 * tokens * width * n * PACK, 8e6),
        name="qkv",
    )(x, gain, weights, table)


def pair_keys(kv):
    other = pltpu.roll(kv, 64, 1)
    low = lane_iota(kv.shape) < 64
    return jnp.where(low, kv, other), jnp.where(low, other, kv)


def stack_heads(q):
    low = lane_iota(q.shape) < 64
    zero = jnp.zeros_like(q)
    return jnp.concatenate([jnp.where(low, q, zero), jnp.where(low, zero, q)], 0)


def fold_heads(stacked):
    rows = stacked.shape[0] // 2
    return jnp.where(lane_iota((rows, 128)) < 64, stacked[:rows], stacked[rows:])


def query_rows(ends_ref, block, length):
    half = length // 2
    lanes = lane_iota((1, 2 * BLK))
    index = block * BLK + jnp.where(lanes < BLK, lanes, lanes - BLK)
    position = jnp.where(index < half, index, length + half - 1 - index)
    start = jnp.zeros_like(position)
    end = 0
    for j in range(3):
        end = end + ends_ref[0, j]
        start = jnp.where(position >= end, jnp.maximum(start, end), start)
    return position, start


def key_position(kb, length):
    half = length // 2
    index = kb * BLK + row_iota((BLK, 1))
    return jnp.where(index < half, index, length + half - 1 - index)


def block_loop(block, per_half, body, init):
    late = block >= per_half
    inner = jnp.where(late, block - per_half, block)

    def plain(kb, carry):
        return body(kb, True, carry)

    def masked(kb, carry):
        return body(kb, False, carry)

    carry = lax.fori_loop(0, jnp.where(late, per_half, inner), plain, init)
    return lax.fori_loop(block, jnp.where(late, 2 * per_half, block + 1), masked, carry)


def attn_forward_kernel(length, ends_ref, q_ref, pack_ref, out_ref, lse_ref, full_ref, keys, values_t, acc):
    block = pl.program_id(0)
    half = length // 2
    n, _, rows, _ = pack_ref.shape

    @pl.when(block == 0)
    def _():
        for h in range(2):
            for c in range(n):
                kk, vv = pair_keys(pack_ref[c, h, :, 128:256].astype(F32))
                at = h * half + c * rows
                keys[at : at + rows, :] = kk.astype(BF16)
                if rows % 128 == 0:
                    values_t[:, at : at + rows] = jnp.transpose(vv).astype(BF16)
        if rows % 128 != 0:
            for h in range(2):
                for c in range(0, n, 2):
                    pair = jnp.concatenate([pack_ref[c, h, :, 128:256], pack_ref[c + 1, h, :, 128:256]], 0)
                    _, vv = pair_keys(pair.astype(F32))
                    at = h * half + c * rows
                    values_t[:, at : at + 2 * rows] = jnp.transpose(vv).astype(BF16)

    q = q_ref[...].reshape(BLK, PACK)[:, :128]
    q2 = stack_heads((q.astype(F32) * ATTN_SCALE).astype(BF16))
    position, start = query_rows(ends_ref, block, length)
    bias = jnp.where(start > 0, MASKED, 0.0)
    acc[...] = jnp.zeros_like(acc)

    def body(kb, whole, carry):
        peak, total = carry
        at = pl.multiple_of(kb * BLK, BLK)
        scores = dot(keys[pl.ds(at, BLK), :], q2, NT)
        if whole:
            scores = scores + bias
        else:
            where = key_position(kb, length)
            scores = jnp.where((where <= position) & (where >= start), scores, MASKED)
        new_peak = jnp.maximum(peak, jnp.max(scores, 0, keepdims=True))
        weights = jnp.exp(scores - new_peak)
        fade = jnp.exp(peak - new_peak)
        total = total * fade + jnp.sum(weights, 0, keepdims=True)
        acc[...] = acc[...] * fade + dot(values_t[:, pl.ds(at, BLK)], weights.astype(BF16))
        return new_peak, total

    init = (jnp.full((1, 2 * BLK), MASKED, F32), jnp.zeros((1, 2 * BLK), F32))
    peak, total = block_loop(block, half // BLK, body, init)
    result = acc[...] / total
    full_ref[0] = result
    lse_ref[0] = peak + jnp.log(total)
    folded = fold_heads(jnp.transpose(result)).astype(BF16)
    out_ref[...] = folded.reshape(out_ref.shape)


def attn_forward(ends, packs, length):
    n, _, rows, _ = packs.shape
    blocks, per = length // BLK, BLK // rows
    per_half = blocks // 2
    tiles = lambda i, ends: (lax.rem(i, per_half), i // per_half, 0, 0)
    return pl.pallas_call(
        functools.partial(attn_forward_kernel, length),
        grid_spec=pltpu.PrefetchScalarGridSpec(
            num_scalar_prefetch=1,
            grid=(blocks,),
            in_specs=[
                pl.BlockSpec((per, 1, rows, PACK), tiles),
                pl.BlockSpec(packs.shape, lambda i, ends: (0, 0, 0, 0)),
            ],
            out_specs=[
                pl.BlockSpec((per, 1, rows, 128), tiles),
                pl.BlockSpec((1, 1, 2 * BLK), lambda i, ends: (i, 0, 0)),
                pl.BlockSpec((1, 128, 2 * BLK), lambda i, ends: (i, 0, 0)),
            ],
            scratch_shapes=[
                pltpu.VMEM((length, 128), BF16),
                pltpu.VMEM((128, length), BF16),
                pltpu.VMEM((128, 2 * BLK), F32),
            ],
        ),
        out_shape=[
            jax.ShapeDtypeStruct((n, 2, rows, 128), BF16),
            jax.ShapeDtypeStruct((blocks, 1, 2 * BLK), F32),
            jax.ShapeDtypeStruct((blocks, 128, 2 * BLK), F32),
        ],
        compiler_params=params(),
        cost_estimate=cost(1.5e10, 6e6),
        name="attn_forward",
    )(ends, packs, packs)


def attn_backward_kernel(length, ends_ref, q_ref, g_ref, pack_ref, lse_ref, full_ref, table_ref, out_ref, keys, values, keys_t, grad_q, grad_k, grad_v, acc):
    block = pl.program_id(0)
    half = length // 2
    n, _, rows, _ = pack_ref.shape

    @pl.when(block == 0)
    def _():
        for h in range(2):
            for c in range(n):
                kk, vv = pair_keys(pack_ref[c, h, :, 128:256].astype(F32))
                at = h * half + c * rows
                keys[at : at + rows, :] = kk.astype(BF16)
                values[at : at + rows, :] = vv.astype(BF16)
        for b in range(length // BLK):
            keys_t[:, b * BLK : (b + 1) * BLK] = jnp.transpose(keys[b * BLK : (b + 1) * BLK, :].astype(F32)).astype(BF16)
        grad_k[...] = jnp.zeros_like(grad_k)
        grad_v[...] = jnp.zeros_like(grad_v)

    q2 = stack_heads((q_ref[...].reshape(BLK, PACK)[:, :128].astype(F32) * ATTN_SCALE).astype(BF16))
    g2 = stack_heads(g_ref[...].reshape(BLK, 128))
    position, start = query_rows(ends_ref, block, length)
    lse = lse_ref[0]
    shift = jnp.where(start > 0, MASKED, 0.0) - lse
    delta = jnp.sum(jnp.transpose(g2.astype(F32)) * full_ref[0], 0, keepdims=True)
    acc[...] = jnp.zeros_like(acc)

    def body(kb, whole, carry):
        at = pl.multiple_of(kb * BLK, BLK)
        scores = dot(keys[pl.ds(at, BLK), :], q2, NT)
        if whole:
            probs = jnp.exp(scores + shift)
        else:
            where = key_position(kb, length)
            probs = jnp.where((where <= position) & (where >= start), jnp.exp(scores - lse), 0.0)
        grad_probs = dot(values[pl.ds(at, BLK), :], g2, NT)
        grad_scores = (probs * (grad_probs - delta)).astype(BF16)
        acc[...] += dot(keys_t[:, pl.ds(at, BLK)], grad_scores)
        grad_k[pl.ds(at, BLK), :] += dot(grad_scores, q2)
        grad_v[pl.ds(at, BLK), :] += dot(probs.astype(BF16), g2)
        return carry

    block_loop(block, half // BLK, body, 0)
    grad_q[pl.ds(pl.multiple_of(block * BLK, BLK), BLK), :] = fold_heads(jnp.transpose(acc[...]))

    @pl.when(block == length // BLK - 1)
    def _():
        for h in range(2):
            for c in range(n):
                at = slice(h * half + c * rows, h * half + (c + 1) * rows)
                kk = grad_k[at, :]
                vv = grad_v[at, :]
                kk = kk + pltpu.roll(kk, 64, 1)
                vv = vv + pltpu.roll(vv, 64, 1)
                both = jnp.where(lane_iota(kk.shape) < 64, kk, vv)
                package = jnp.concatenate([grad_q[at, :] * ATTN_SCALE, both], -1)
                out_ref[c, h] = turn(package, table_ref[at, :], -1.0).astype(BF16)


def attn_backward(ends, packs, grads, lse, full, table, length):
    n, _, rows, _ = packs.shape
    blocks, per = length // BLK, BLK // rows
    per_half = blocks // 2
    tiles = lambda i, ends: (lax.rem(i, per_half), i // per_half, 0, 0)
    return pl.pallas_call(
        functools.partial(attn_backward_kernel, length),
        grid_spec=pltpu.PrefetchScalarGridSpec(
            num_scalar_prefetch=1,
            grid=(blocks,),
            in_specs=[
                pl.BlockSpec((per, 1, rows, PACK), tiles),
                pl.BlockSpec((per, 1, rows, 128), tiles),
                pl.BlockSpec(packs.shape, lambda i, ends: (0, 0, 0, 0)),
                pl.BlockSpec((1, 1, 2 * BLK), lambda i, ends: (i, 0, 0)),
                pl.BlockSpec((1, 128, 2 * BLK), lambda i, ends: (i, 0, 0)),
                pl.BlockSpec(table.shape, lambda i, ends: (0, 0)),
            ],
            out_specs=pl.BlockSpec(packs.shape, lambda i, ends: (0, 0, 0, 0)),
            scratch_shapes=[
                pltpu.VMEM((length, 128), BF16),
                pltpu.VMEM((length, 128), BF16),
                pltpu.VMEM((128, length), BF16),
                pltpu.VMEM((length, 128), F32),
                pltpu.VMEM((length, 128), F32),
                pltpu.VMEM((length, 128), F32),
                pltpu.VMEM((128, 2 * BLK), F32),
            ],
        ),
        out_shape=jax.ShapeDtypeStruct(packs.shape, BF16),
        compiler_params=params(),
        cost_estimate=cost(3e10, 8e6),
        name="attn_backward",
    )(ends, packs, grads, packs, lse, full, table)


def middle_kernel(attn_ref, wo_ref, x_ref, gain_ref, middle_ref, h_ref):
    total = None
    for c in range(attn_ref.shape[0]):
        part = dot(attn_ref[c], wo_ref[c])
        total = part if total is None else total + part
    middle = x_ref[...] + RESIDUAL * total
    middle_ref[...] = middle
    normed, _ = norm_parts(middle)
    h_ref[...] = (normed * gain_ref[...]).astype(BF16)


def middle_step(attn, wo, x, gain):
    tokens, width = x.shape
    return pl.pallas_call(
        middle_kernel,
        out_shape=[jax.ShapeDtypeStruct((tokens, width), F32), jax.ShapeDtypeStruct((tokens, width), BF16)],
        compiler_params=params(),
        cost_estimate=cost(2 * tokens * width * width, 5e6),
        name="middle",
    )(attn, wo, x, gain)


def own_row(table, row):
    return jnp.sum(jnp.where(row_iota(table.shape) == row, table, 0.0), 0, keepdims=True)


def one_hot(slots, first, number, capp):
    tokens = slots.shape[1]
    order = row_iota((capp, tokens)).astype(F32)
    return [(order == own_row(slots, first + j)).astype(F32) for j in range(number)]


def gather_kernel(number, capp, first_ref, h_ref, cx_ref, wrt_ref, x_ref, g_ref, gate_ref):
    tokens = h_ref.shape[1]
    first = first_ref[0]
    h = h_ref[0]
    slots = cx_ref[0, tokens:, :tokens].astype(F32)
    logits = dot(wrt_ref[...], h, NT)[:EXPERTS, :]
    raw = jnp.exp(logits - jnp.max(logits, 0, keepdims=True))
    router = raw / jnp.sum(raw, 0, keepdims=True)
    hots = one_hot(slots, first, number, capp)
    places = jnp.concatenate(hots, 0).astype(BF16)
    rows = dot(places, h).astype(BF16)
    grads = dot(places, cx_ref[0, :tokens, :]).astype(BF16)
    for j in range(number):
        at = slice(j * capp, (j + 1) * capp)
        x_ref[j, 0] = rows[at]
        g_ref[j, 0] = grads[at]
        gate = jnp.sum(hots[j] * own_row(router, first + j), 1, keepdims=True)
        gate_ref[j, 0] = jnp.broadcast_to(gate, (capp, 128))


def gather_rows(first, hs, cxs, wrt, number, capp):
    nb, tokens, width = hs.shape
    return pl.pallas_call(
        functools.partial(gather_kernel, number, capp),
        grid_spec=pltpu.PrefetchScalarGridSpec(
            num_scalar_prefetch=1,
            grid=(nb,),
            in_specs=[
                pl.BlockSpec((1, tokens, width), lambda b, f: (b, 0, 0)),
                pl.BlockSpec((1, tokens + EXPERTS, width), lambda b, f: (b, 0, 0)),
                pl.BlockSpec(wrt.shape, lambda b, f: (0, 0)),
            ],
            out_specs=[
                pl.BlockSpec((number, 1, capp, width), lambda b, f: (0, b, 0, 0)),
                pl.BlockSpec((number, 1, capp, width), lambda b, f: (0, b, 0, 0)),
                pl.BlockSpec((number, 1, capp, 128), lambda b, f: (0, b, 0, 0)),
            ],
        ),
        out_shape=[
            jax.ShapeDtypeStruct((number, nb, capp, width), BF16),
            jax.ShapeDtypeStruct((number, nb, capp, width), BF16),
            jax.ShapeDtypeStruct((number, nb, capp, 128), F32),
        ],
        compiler_params=params(),
        cost_estimate=cost(4 * nb * number * capp * tokens * width, 2e7),
        name="gather_rows",
    )(first, hs, cxs, wrt)


PIECE = 512


def expert_kernel(base_ref, x_ref, g_ref, gate_ref, wg_ref, wu_ref, wd_ref, piece_ref, out_ref, rows_ref, dg_ref):
    x = x_ref[0]
    gate = gate_ref[0][:, :1]
    grad_ffn = RESIDUAL * g_ref[0].astype(F32)
    go = (gate * grad_ffn).astype(BF16)
    part = wg_ref.shape[2] // 2
    out = rows = None
    for chunk in range(2):
        at = slice(chunk * part, (chunk + 1) * part)
        wg, wu, wd = wg_ref[0, :, at], wu_ref[0, :, at], wd_ref[0, at, :]
        pre_gate = dot(x, wg)
        pre_up = dot(x, wu)
        sig = jax.nn.sigmoid(pre_gate)
        hidden = (pre_gate * sig * pre_up).astype(BF16)
        out_part = dot(hidden, wd)
        grad_hidden = dot(go, wd, NT)
        grad_gate = (grad_hidden * pre_up * sig * (1.0 + pre_gate * (1.0 - sig))).astype(BF16)
        grad_up = (grad_hidden * pre_gate * sig).astype(BF16)
        row_part = dot(grad_gate, wg, NT) + dot(grad_up, wu, NT)
        dwg = dot(x, grad_gate, TN).astype(BF16)
        dwu = dot(x, grad_up, TN).astype(BF16)
        dwd = dot(hidden, go, TN).astype(BF16)
        for half in range(2):
            side = slice(half * PIECE, (half + 1) * PIECE)
            piece_ref[0, 3 * chunk + half, :, :part] = dwg[side]
            piece_ref[0, 3 * chunk + half, :, part:] = dwu[side]
            piece_ref[0, 3 * chunk + 2, half * part : (half + 1) * part, :] = dwd[:, side]
        out = out_part if out is None else out + out_part
        rows = row_part if rows is None else rows + row_part
    out = out.astype(BF16).astype(F32)
    out_ref[0] = (gate * out).astype(BF16)
    rows_ref[0] = rows.astype(BF16)
    grad = jnp.sum(grad_ffn * out, 1, keepdims=True)
    dg_ref[0] = jnp.broadcast_to(grad, dg_ref.shape[1:])


def expert_step(base, xs, gs, gates, w_gate, w_up, w_down):
    number, rows, width = xs.shape
    ff = w_gate.shape[2]
    row = lambda e, b: (e, 0, 0)
    weight = lambda e, b: (b[0] + e, 0, 0)
    return pl.pallas_call(
        expert_kernel,
        grid_spec=pltpu.PrefetchScalarGridSpec(
            num_scalar_prefetch=1,
            grid=(number,),
            in_specs=[
                pl.BlockSpec((1, rows, width), row),
                pl.BlockSpec((1, rows, width), row),
                pl.BlockSpec((1, rows, 128), row),
                pl.BlockSpec((1, width, ff), weight),
                pl.BlockSpec((1, width, ff), weight),
                pl.BlockSpec((1, ff, width), weight),
            ],
            out_specs=[
                pl.BlockSpec((1, 6, PIECE, PIECE), lambda e, b: (e, 0, 0, 0)),
                pl.BlockSpec((1, rows, width), row),
                pl.BlockSpec((1, rows, width), row),
                pl.BlockSpec((1, rows, 128), row),
            ],
        ),
        out_shape=[
            jax.ShapeDtypeStruct((number, 6, PIECE, PIECE), BF16),
            jax.ShapeDtypeStruct((number, rows, width), BF16),
            jax.ShapeDtypeStruct((number, rows, width), BF16),
            jax.ShapeDtypeStruct((number, rows, 128), F32),
        ],
        compiler_params=params(60),
        cost_estimate=cost(18 * number * rows * width * ff, 5e7),
        name="expert_step",
    )(base, xs, gs, gates, w_gate, w_up, w_down)


def combine_kernel(number, capp, first_ref, slot_ref, outs, rows, grads, y_ref, gx_ref):
    tokens = y_ref.shape[1]
    width = y_ref.shape[2]
    first = first_ref[0]
    slots = slot_ref[0][:, :tokens].astype(F32)
    hots = one_hot(slots, first, number, capp)
    places = jnp.concatenate(hots, 0).astype(BF16)
    y_ref[0] = dot(places, outs[:, 0].reshape(number * capp, width), TN).astype(BF16)
    gx_ref[0, :tokens] = dot(places, rows[:, 0].reshape(number * capp, width), TN).astype(BF16)
    extra = jnp.zeros((EXPERTS, 2 * tokens), F32)
    for j in range(number):
        grad = jnp.sum(hots[j] * grads[j, 0][:, :1], 0, keepdims=True)
        high = grad.astype(BF16).astype(F32)
        both = jnp.concatenate([high, grad - high], 1)
        extra = jnp.where(row_iota(extra.shape) == first + j, both, extra)
    rest = jnp.zeros((EXPERTS, width - 2 * tokens), F32)
    gx_ref[0, tokens:] = jnp.concatenate([extra, rest], 1).astype(BF16)


def combine(first, slots, outs, rows, grads, tokens, capp):
    number = outs.shape[0]
    nb, _, width = slots.shape
    split = lambda a: a.reshape(number, nb, capp, a.shape[-1])
    wide = pl.BlockSpec((number, 1, capp, width), lambda b, f: (0, b, 0, 0))
    thin = pl.BlockSpec((number, 1, capp, 128), lambda b, f: (0, b, 0, 0))
    return pl.pallas_call(
        functools.partial(combine_kernel, number, capp),
        grid_spec=pltpu.PrefetchScalarGridSpec(
            num_scalar_prefetch=1,
            grid=(nb,),
            in_specs=[pl.BlockSpec((1, EXPERTS, width), lambda b, f: (b, 0, 0))] + [wide, wide, thin],
            out_specs=[
                pl.BlockSpec((1, tokens, width), lambda b, f: (b, 0, 0)),
                pl.BlockSpec((1, tokens + EXPERTS, width), lambda b, f: (b, 0, 0)),
            ],
        ),
        out_shape=[
            jax.ShapeDtypeStruct((nb, tokens, width), BF16),
            jax.ShapeDtypeStruct((nb, tokens + EXPERTS, width), BF16),
        ],
        compiler_params=params(),
        cost_estimate=cost(4 * nb * number * capp * tokens * width, 2e7),
        name="combine",
    )(first, slots, split(outs), split(rows), split(grads))


def home_kernel(gx_ref, h_ref, middle_ref, cot_ref, wr_ref, wo_ref, gain_ref, attn_ref, grad_middle_ref, dwo_ref, ga_ref, dwr_ref, dgain_ref):
    tokens, width = h_ref.shape
    h = h_ref[...]
    gain = gain_ref[...]
    extra = gx_ref[tokens:, :].astype(F32)
    grad_router = extra[:, :tokens] + extra[:, tokens : 2 * tokens]
    grad_router = jnp.transpose(jnp.concatenate([grad_router, jnp.zeros((128 - EXPERTS, tokens), F32)], 0))
    logits = dot(h, wr_ref[...])
    logits = jnp.where(lane_iota(logits.shape) < EXPERTS, logits, MASKED)
    raw = jnp.exp(logits - jnp.max(logits, -1, keepdims=True))
    router = raw / jnp.sum(raw, -1, keepdims=True)
    grad_logits = (router * (grad_router - jnp.sum(router * grad_router, -1, keepdims=True))).astype(BF16)
    dwr_ref[...] = dot(h, grad_logits, TN).astype(BF16)
    grad_h = gx_ref[:tokens, :].astype(F32) + dot(grad_logits, wr_ref[...], NT)
    normed, scale = norm_parts(middle_ref[...])
    dgain_ref[...] = jnp.sum(grad_h * normed, 0, keepdims=True)
    grad_middle = cot_ref[...] + norm_back(grad_h * gain, normed, scale)
    grad_middle_ref[...] = grad_middle
    grad_branch = (RESIDUAL * grad_middle).astype(BF16)
    for c in range(attn_ref.shape[0]):
        dwo_ref[c] = dot(attn_ref[c], grad_branch, TN).astype(BF16)
        ga_ref[c] = dot(grad_branch, wo_ref[c], NT).astype(BF16)


def home_step(gx, h, middle, cot, wr, wo, gain, attn):
    tokens, width = h.shape
    n = attn.shape[0]
    return pl.pallas_call(
        home_kernel,
        out_shape=[
            jax.ShapeDtypeStruct((tokens, width), F32),
            jax.ShapeDtypeStruct((n, 128, width), BF16),
            jax.ShapeDtypeStruct((n, tokens, 128), BF16),
            jax.ShapeDtypeStruct((width, 128), BF16),
            jax.ShapeDtypeStruct((1, width), F32),
        ],
        compiler_params=params(),
        cost_estimate=cost(4 * tokens * width * width, 1e7),
        name="home_step",
    )(gx, h, middle, cot, wr, wo, gain, attn)


def final_kernel(shard, grads_ref, w_ref, h_ref, x_ref, gain_ref, grad_middle_ref, dw_ref, grad_x_ref, dgain_ref, total):
    c = pl.program_id(0)
    g = grads_ref[0]
    dw_ref[...] = dot(h_ref[...], g, TN).astype(BF16)

    @pl.when(c == 0)
    def _():
        total[...] = jnp.zeros_like(total)

    for f in range(w_ref.shape[0]):
        total[:, f * shard : (f + 1) * shard] += dot(g, w_ref[f, :shard, :], NT)

    @pl.when(c == pl.num_programs(0) - 1)
    def _():
        normed, scale = norm_parts(x_ref[...])
        grad_h = total[...]
        dgain_ref[...] = jnp.sum(grad_h * normed, 0, keepdims=True)
        grad_x_ref[...] = grad_middle_ref[...] + norm_back(grad_h * gain_ref[...], normed, scale)


def final_step(grads, weights, h, x, gain, grad_middle, shard):
    n, tokens, _ = grads.shape
    width = x.shape[1]
    fsdp, padded, _ = weights.shape
    same = lambda c: (0, 0)
    return pl.pallas_call(
        functools.partial(final_kernel, shard),
        grid=(n,),
        in_specs=[
            pl.BlockSpec((1, tokens, PACK), lambda c: (c, 0, 0)),
            pl.BlockSpec((fsdp, padded, PACK), lambda c: (0, 0, c)),
            pl.BlockSpec((tokens, width), same),
            pl.BlockSpec((tokens, width), same),
            pl.BlockSpec((1, width), same),
            pl.BlockSpec((tokens, width), same),
        ],
        out_specs=[
            pl.BlockSpec((width, PACK), lambda c: (0, c)),
            pl.BlockSpec((tokens, width), same),
            pl.BlockSpec((1, width), same),
        ],
        out_shape=[
            jax.ShapeDtypeStruct((width, n * PACK), BF16),
            jax.ShapeDtypeStruct((tokens, width), F32),
            jax.ShapeDtypeStruct((1, width), F32),
        ],
        scratch_shapes=[pltpu.VMEM((tokens, width), F32)],
        compiler_params=params(),
        cost_estimate=cost(4 * tokens * width * n * PACK, 1.2e7),
        name="final_step",
    )(grads, weights, h, x, gain, grad_middle)


def widen_kernel(number, index_ref, own_ref, other_ref, gate_ref, up_ref, down_ref):
    part = gate_ref.shape[2] // 2

    def write(ref):
        for chunk in range(2):
            columns = slice(chunk * part, (chunk + 1) * part)
            for half in range(2):
                at = slice(half * PIECE, (half + 1) * PIECE)
                gate_ref[0, at, columns] = ref[3 * chunk + half, :, :part].astype(F32)
                up_ref[0, at, columns] = ref[3 * chunk + half, :, part:].astype(F32)
                down_ref[0, columns, at] = ref[3 * chunk + 2, half * part : (half + 1) * part, :].astype(F32)

    @pl.when(pl.program_id(0) == 0)
    def _():
        write(own_ref)

    @pl.when(pl.program_id(0) == 1)
    def _():
        write(other_ref)


def tail_kernel(number, index_ref, own_ref, other_ref, own_small_ref, other_small_ref, mixed_in, grad_in, gate_ref, up_ref, down_ref, mixed_ref, grad_ref, dwq_ref, dwk_ref, dwv_ref, dwo_ref, dwr_ref, g1_ref, g2_ref):
    widen_kernel(number, index_ref, own_ref, other_ref, gate_ref, up_ref, down_ref)
    mixed_ref[...] = mixed_in[...]
    grad_ref[...] = grad_in[...]

    @pl.when((pl.program_id(0) == 0) & (pl.program_id(1) == 0))
    def _():
        for which, ref in enumerate((own_small_ref, other_small_ref)):
            part = index_ref[which] // number
            at = pl.ds(pl.multiple_of(part * 128, 128), 128)
            for q in range(4):
                block = ref[1, q * 128 : (q + 1) * 128, :].astype(F32)
                dwq_ref[at, q * 256 : q * 256 + 128] = block[:, :128]
                dwq_ref[at, q * 256 + 128 : (q + 1) * 256] = block[:, 256:384]
                one, two = block[:, 128:256], block[:, 384:]
                low = lane_iota(one.shape) < HEAD_DIMENSION
                dwk_ref[at, q * 128 : (q + 1) * 128] = jnp.where(low, one, pltpu.roll(two, 64, 1))
                dwv_ref[at, q * 128 : (q + 1) * 128] = jnp.where(low, pltpu.roll(one, 64, 1), two)
            dwo_ref[at, :PIECE] = ref[0, 0:128, :].astype(F32)
            dwo_ref[at, PIECE:] = ref[0, 128:256, :].astype(F32)
            dwr_ref[:, at] = jnp.transpose(ref[0, 256:384, :128].astype(F32))[:EXPERTS]
            gains = ref[0, 384:400, :128].astype(F32)
            g1_ref[pl.ds(part, 1), :] = gains[0:1]
            g2_ref[pl.ds(part, 1), :] = gains[1:2]


def expert_specs(number, shapes):
    last = number - 1
    ins = [
        pl.BlockSpec((6, PIECE, PIECE), lambda s, e, at: (jnp.where(s == 0, e, last), 0, 0)),
        pl.BlockSpec((6, PIECE, PIECE), lambda s, e, at: (jnp.where(s == 0, 0, e), 0, 0)),
    ]
    outs = [pl.BlockSpec((1,) + tuple(shape[1:]), lambda s, e, at: (at[s] + e, 0, 0)) for shape in shapes]
    return ins, outs, [jax.ShapeDtypeStruct(shape, F32) for shape in shapes]


def widen(index, own, other, shapes):
    number = shapes[0][0] // 2
    ins, outs, out_shapes = expert_specs(number, shapes)
    return pl.pallas_call(
        functools.partial(widen_kernel, number),
        grid_spec=pltpu.PrefetchScalarGridSpec(num_scalar_prefetch=1, grid=(2, number), in_specs=ins, out_specs=outs),
        out_shape=out_shapes,
        compiler_params=params(),
        cost_estimate=cost(0, 1e8),
        name="widen",
    )(index, own, other)


def tail(index, own, other, mixed, grad_x, shapes, shard):
    number = shapes[0][0] // 2
    tokens, width = mixed.shape
    ins, outs, out_shapes = expert_specs(number, shapes)
    small = pl.BlockSpec((2, PIECE, PIECE), lambda s, e, at: (3 * number, 0, 0))
    rows = pl.BlockSpec((tokens // (2 * number), width), lambda s, e, at: (s * number + e, 0))
    small_shapes = [(shard, width), (shard, width // 2), (shard, width // 2), (shard, width), (EXPERTS, shard), (2, 128), (2, 128)]
    whole = [pl.BlockSpec(shape, lambda s, e, at: (0, 0)) for shape in small_shapes]
    return pl.pallas_call(
        functools.partial(tail_kernel, number),
        grid_spec=pltpu.PrefetchScalarGridSpec(
            num_scalar_prefetch=1,
            grid=(2, number),
            in_specs=ins + [small, small, rows, rows],
            out_specs=outs + [rows, rows] + whole,
        ),
        out_shape=out_shapes
        + [jax.ShapeDtypeStruct((tokens, width), F32)] * 2
        + [jax.ShapeDtypeStruct(shape, F32) for shape in small_shapes],
        compiler_params=params(),
        cost_estimate=cost(0, 1e8),
        name="tail",
    )(index, own, other, own, other, mixed, grad_x)


def swap(value, axis, bit):
    size = lax.axis_size(axis)
    return lax.ppermute(value, axis, [(i, i ^ bit) for i in range(size)])


def group_bits(fsdp):
    bits = [("fsdp", 1 << b) for b in range(1, fsdp.bit_length() - 1)]
    return bits + [("ctx", 1), ("fsdp", 1)]


def group_gather(value, bits):
    stacked = value[None]
    for axis, bit in bits:
        stacked = jnp.concatenate([stacked, swap(stacked, axis, bit)], 0)
    return stacked


def group_reduce(stacked, bits):
    for axis, bit in reversed(bits):
        half = stacked.shape[0] // 2
        arrived = swap(stacked[half:], axis, bit)
        stacked = (stacked[:half].astype(F32) + arrived.astype(F32)).astype(stacked.dtype)
    return stacked[0]


def line_sum(value, ctx):
    pairs = ctx // 2
    if pairs != 4:
        bit = 2
        while bit < ctx:
            value = value + swap(value, "ctx", bit)
            bit *= 2
        return value
    at = lambda z, y: 2 * z + y
    inward = [(at(0, y), at(1, y)) for y in range(2)] + [(at(3, y), at(2, y)) for y in range(2)]
    across = [(at(1, y), at(2, y)) for y in range(2)] + [(at(2, y), at(1, y)) for y in range(2)]
    outward = [(b, a) for a, b in inward]
    value = value + lax.ppermute(value, "ctx", inward)
    value = value + lax.ppermute(value, "ctx", across)
    arrived = lax.ppermute(value, "ctx", outward)
    z = lax.axis_index("ctx") // 2
    return jnp.where((z == 0) | (z == 3), arrived, value)


MESH = pl.DeviceIdType.MESH


def flip(index, bit):
    return jnp.where((index // bit) % 2 == 0, index + bit, index - bit)


def send(src, dst, send_sem, recv_sem, device):
    return pltpu.make_async_remote_copy(src_ref=src, dst_ref=dst, send_sem=send_sem, recv_sem=recv_sem, device_id=device, device_id_type=MESH)


def neighbours():
    ctx, fsdp = lax.axis_index("ctx"), lax.axis_index("fsdp")
    side, across = flip(ctx, 1), flip(fsdp, 2)
    core = {"fsdp": flip(fsdp, 1)}
    return core, [{"fsdp": across}, {"ctx": side}, {"ctx": side, "fsdp": across}]


def greet(devices):
    barrier = pltpu.get_barrier_semaphore()
    for device in devices:
        pl.semaphore_signal(barrier, inc=1, device_id=device, device_id_type=MESH)
    pl.semaphore_wait(barrier, len(devices))


def others(n):
    ctx = lax.axis_index("ctx")
    return [lax.rem(ctx + d, n) for d in range(1, n)]


def exchange_start(src, dst, send_sems, recv_sems, local_sem, n):
    ctx = lax.axis_index("ctx")
    for d, c in enumerate(others(n)):
        send(src.at[c], dst.at[ctx], send_sems.at[d], recv_sems.at[d], {"ctx": c}).start()
    pltpu.make_async_copy(src.at[ctx], dst.at[ctx], local_sem).start()


def exchange_wait(src, dst, send_sems, recv_sems, local_sem, n, arrived=None):
    ctx = lax.axis_index("ctx")
    pltpu.make_async_copy(src.at[ctx], dst.at[ctx], local_sem).wait()
    if arrived is not None:
        arrived(ctx)
    for d in range(n - 1):
        source = lax.rem(ctx + n - 1 - d, n)
        send(src.at[source], dst.at[source], send_sems.at[d], recv_sems.at[d], {"ctx": source}).wait_recv()
        if arrived is not None:
            arrived(source)
    for d, c in enumerate(others(n)):
        send(src.at[c], dst.at[ctx], send_sems.at[d], recv_sems.at[d], {"ctx": c}).wait_send()


def turn_half(v, table, direction, lanes_turned):
    lanes = lane_iota(v.shape)
    swapped = jnp.where(lanes % HEAD_DIMENSION < HEAD_DIMENSION // 2, pltpu.roll(v, 96, 1), pltpu.roll(v, 32, 1))
    return jnp.where(lanes < lanes_turned, v * table[:, :128] + direction * (swapped * table[:, 128:]), v)


def front_kernel(n, cap, wq_ref, wk_ref, wv_ref, wo_part_ref, wr_raw_ref, gain_ref, x_ref, table_ref, routes_ref, cot_ref, packs_ref, h_ref, weights_ref, wo_ref, wr_ref, cxs_ref, gains_ref, wall, packed_ref, wr_part_ref, cx, table, normed_ref, total, out, exch_send, exch_recv, full_send, full_recv, x_send, x_recv, y_send, y_recv, xs_send, xs_recv, ys_send, ys_recv, cx_send, cx_recv, local_sems):
    tokens, width = x_ref.shape
    shard = width // 4
    ctx, fsdp = lax.axis_index("ctx"), lax.axis_index("fsdp")
    parity = lax.rem(ctx, 2)
    core, group = neighbours()
    far, near = group[0], group[1]
    sibling, distant = flip(fsdp, 1), flip(fsdp, 2)
    other = flip(distant, 1)
    for k in range(2):
        pltpu.make_async_copy(table_ref.at[k, ctx], table.at[k], local_sems.at[6 + k]).start()

    pair = HEAD_DIMENSION * 2
    for c in range(0, n, 2):
        keys, values = wk_ref[:, c // 2 * pair : (c // 2 + 1) * pair].astype(F32), wv_ref[:, c // 2 * pair : (c // 2 + 1) * pair].astype(F32)
        low = lane_iota(keys.shape) < HEAD_DIMENSION
        packed_ref[0, :shard, c * 128 : (c + 1) * 128] = jnp.where(low, keys, pltpu.roll(values, 64, 1)).astype(BF16)
        packed_ref[0, :shard, (c + 1) * 128 : (c + 2) * 128] = jnp.where(low, pltpu.roll(keys, 64, 1), values).astype(BF16)
    below = packed_ref.shape[1] - shard
    packed_ref[0, shard:, :] = jnp.zeros((below, width), BF16)
    row = row_iota((16, shard))
    gains = gain_ref[...].astype(F32)
    gain_rows = jnp.where(row == 0, gains[0:1], jnp.where(row == 1, gains[1:2], 0.0))
    packed_ref[0, shard : shard + 16, :shard] = gain_rows.astype(BF16)
    packed_ref[1, :shard, :] = wq_ref[...]
    packed_ref[1, shard:, :] = jnp.zeros((below, width), BF16)
    router = jnp.concatenate([wr_raw_ref[...].astype(F32), jnp.zeros((128 - EXPERTS, shard), F32)], 0)
    wr_part_ref[...] = jnp.transpose(router).astype(BF16)
    greet([core, far] + [{"ctx": c} for c in others(n)])

    half_rows = packed_ref.shape[1] // 2

    def cut(k, part):
        if k < 2:
            return pl.ds(pl.multiple_of(part * half_rows, 16), half_rows)
        if k == 2:
            return pl.ds(part, 1)
        return pl.ds(pl.multiple_of(part * (shard // 2), 16), shard // 2)

    sources = [packed_ref.at[0], packed_ref.at[1], wo_part_ref, wr_part_ref]
    targets = [wall.at[0], wall.at[1], wo_ref, wr_ref]

    def whole(k):
        return send(sources[k], targets[k].at[fsdp], full_send.at[k], full_recv.at[k], core)

    def own(k):
        return pltpu.make_async_copy(sources[k], targets[k].at[fsdp], local_sems.at[k])

    def to_far(k):
        return send(sources[k].at[cut(k, parity)], targets[k].at[fsdp, cut(k, parity)], x_send.at[k], x_recv.at[k], far)

    def pass_on(k, part, sems, device):
        ref = targets[k].at[distant, cut(k, part)]
        return send(ref, ref, sems[0].at[k], sems[1].at[k], device)

    def sibling_arrived(k):
        ref = targets[k].at[sibling]
        send(ref, ref, full_send.at[k], full_recv.at[k], core).wait_recv()

    def far_arrived(k):
        ref = targets[k].at[distant, cut(k, parity)]
        send(ref, ref, x_send.at[k], x_recv.at[k], far).wait_recv()
        pass_on(k, parity, (y_send, y_recv), near).start()
        pass_on(k, parity, (xs_send, xs_recv), core).start()

    def near_arrived(k):
        pass_on(k, 1 - parity, (y_send, y_recv), near).wait_recv()
        pass_on(k, 1 - parity, (ys_send, ys_recv), core).start()

    def core_arrived(k):
        for part, sems in ((parity, (xs_send, xs_recv)), (1 - parity, (ys_send, ys_recv))):
            ref = targets[k].at[other, cut(k, part)]
            send(ref, ref, sems[0].at[k], sems[1].at[k], core).wait_recv()

    for k in range(2):
        to_far(k).start()
    for k in range(2):
        whole(k).start()
        own(k).start()

    prep_kernel(cap, routes_ref, cot_ref, cx)
    pltpu.make_async_copy(cx, cxs_ref.at[0], local_sems.at[4]).start()
    normed, _ = norm_parts(x_ref[...])
    normed_ref[...] = normed

    def project(k, block, begin):
        at = pl.ds(pl.multiple_of(block * shard, shard), shard)
        if k == 0:
            gain = wall[0, block, shard : shard + 16, :shard].astype(F32)
            gains_ref[:, at] = gain
            h_ref[:, at] = (normed_ref[:, at] * gain[:1]).astype(BF16)
        part = dot(h_ref[:, at], wall[k, block, :shard, :])
        total[k] = part if begin else total[k] + part

    for k in range(2):
        own(k).wait()
        project(k, fsdp, True)
        sibling_arrived(k)
        project(k, sibling, False)
        if k == 0:
            far_arrived(0)

    exchanges = []

    def emit(k):
        lanes = slice(128, 256) if k == 0 else slice(0, 128)
        for c in range(n):
            out[c, :, lanes] = turn_half(total[k, :, c * 128 : (c + 1) * 128], angles, 1.0, 64 if k == 0 else 128).astype(BF16)
        cut_lanes = pl.ds(128 if k == 0 else 0, 128)
        source, target = out.at[:, :, cut_lanes], packs_ref.at[:, :, cut_lanes]
        exchanges.append((source, target, exch_send.at[k], exch_recv.at[k], local_sems.at[8 + k], n))
        exchange_start(*exchanges[-1])

    near_arrived(0)
    project(0, distant, False)
    core_arrived(0)
    project(0, other, False)
    for k in range(2):
        pltpu.make_async_copy(table_ref.at[k, ctx], table.at[k], local_sems.at[6 + k]).wait()
    angles = table[...].reshape(tokens, 256)
    emit(0)
    far_arrived(1)
    for k in (2, 3):
        own(k).start()
        whole(k).start()
        to_far(k).start()
    send(cx, cxs_ref.at[1], cx_send.at[0], cx_recv.at[0], far).start()
    near_arrived(1)
    project(1, distant, False)
    core_arrived(1)
    project(1, other, False)
    emit(1)
    keep = pltpu.make_async_copy(wall, weights_ref, local_sems.at[5])
    keep.start()
    for k in (2, 3):
        far_arrived(k)
    for k in (2, 3):
        near_arrived(k)
    for k in (2, 3):
        core_arrived(k)
        sibling_arrived(k)
        own(k).wait()
    for exchange in exchanges:
        exchange_wait(*exchange)
    for k in range(4):
        whole(k).wait_send()
        to_far(k).wait_send()
        pass_on(k, parity, (y_send, y_recv), near).wait_send()
        pass_on(k, parity, (xs_send, xs_recv), core).wait_send()
        pass_on(k, 1 - parity, (ys_send, ys_recv), core).wait_send()
    send(cx, cxs_ref.at[1], cx_send.at[0], cx_recv.at[0], far).wait()
    pltpu.make_async_copy(cx, cxs_ref.at[0], local_sems.at[4]).wait()
    keep.wait()


def front(wq, wk, wv, wo_part, wr, gains, x, table, routes, cot, cap, n):
    tokens, width = x.shape
    shard = wq.shape[0]
    hbm, vmem = pl.BlockSpec(memory_space=pl.ANY), pl.BlockSpec(memory_space=pltpu.VMEM)
    dma = lambda *k: pltpu.SemaphoreType.DMA(k)
    shaped = lambda shape, dtype=BF16: jax.ShapeDtypeStruct(shape, dtype)
    cx_shape = (tokens + EXPERTS, width)
    padded = 2 * 16 * (shard // 32 + 1)
    return pl.pallas_call(
        functools.partial(front_kernel, n, cap),
        in_specs=[vmem, vmem, vmem, hbm, vmem, vmem, vmem, hbm, vmem, vmem],
        out_specs=[hbm, vmem, hbm, hbm, hbm, hbm, vmem],
        out_shape=[
            shaped((n, tokens, PACK)),
            shaped((tokens, width)),
            shaped((2, 4, padded, width)),
            shaped((4,) + wo_part.shape),
            shaped((4, shard, 128)),
            shaped((2,) + cx_shape),
            shaped((16, width), F32),
        ],
        scratch_shapes=[
            pltpu.VMEM((2, 4, padded, width), BF16),
            pltpu.VMEM((2, padded, width), BF16),
            pltpu.VMEM((shard, 128), BF16),
            pltpu.VMEM(cx_shape, BF16),
            pltpu.VMEM((2, tokens // 2, 256), F32),
            pltpu.VMEM((tokens, width), F32),
            pltpu.VMEM((2, tokens, width), F32),
            pltpu.VMEM((n, tokens, PACK), BF16),
            dma(2, n - 1),
            dma(2, n - 1),
        ]
        + [dma(4)] * 10
        + [dma(1), dma(1), dma(10)],
        compiler_params=params(collective_id=1, has_side_effects=True),
        cost_estimate=cost(2e9, 5e7),
        name="front",
    )(wq, wk, wv, wo_part, wr, gains, x, table, routes, cot)


def attend_kernel(length, n, ends_ref, q_ref, pack_ref, cxs_ref, out_ref, lse_ref, full_ref, rest_ref, keys, values_t, acc, near_send, near_recv, core_send, core_recv):
    block = pl.program_id(0)
    core, group = neighbours()
    near = group[1]

    def to_near():
        return send(cxs_ref.at[0], rest_ref.at[0], near_send.at[0], near_recv.at[0], near)

    def to_core(i):
        src = cxs_ref.at[i] if i < 2 else rest_ref.at[0]
        return send(src, rest_ref.at[1 + i], core_send.at[i], core_recv.at[i], core)

    @pl.when(block == 0)
    def _():
        greet([core, near])
        to_near().start()
        for i in range(2):
            to_core(i).start()

    attn_forward_kernel(length, ends_ref, q_ref, pack_ref, out_ref, lse_ref, full_ref, keys, values_t, acc)

    @pl.when(block == pl.num_programs(0) - 2)
    def _():
        to_near().wait_recv()
        to_core(2).start()

    @pl.when(block == pl.num_programs(0) - 1)
    def _():
        for i in range(3):
            to_core(i).wait()
        to_near().wait_send()


def attend(ends, packs, cxs, length):
    n, _, rows, _ = packs.shape
    blocks, per = length // BLK, BLK // rows
    per_half = blocks // 2
    tiles = lambda i: (lax.rem(i, per_half), i // per_half, 0, 0)
    hbm = pl.BlockSpec(memory_space=pl.ANY)
    dma = lambda k: pltpu.SemaphoreType.DMA((k,))
    return pl.pallas_call(
        functools.partial(attend_kernel, length, n),
        grid=(blocks,),
        in_specs=[
            pl.BlockSpec(memory_space=pltpu.SMEM),
            pl.BlockSpec((per, 1, rows, PACK), tiles),
            pl.BlockSpec(packs.shape, lambda i: (0, 0, 0, 0)),
            hbm,
        ],
        out_specs=[
            pl.BlockSpec((per, 1, rows, 128), tiles),
            pl.BlockSpec((1, 1, 2 * BLK), lambda i: (i, 0, 0)),
            pl.BlockSpec((1, 128, 2 * BLK), lambda i: (i, 0, 0)),
            hbm,
        ],
        scratch_shapes=[
            pltpu.VMEM((length, 128), BF16),
            pltpu.VMEM((128, length), BF16),
            pltpu.VMEM((128, 2 * BLK), F32),
            dma(1),
            dma(1),
            dma(3),
            dma(3),
        ],
        out_shape=[
            jax.ShapeDtypeStruct((n, 2, rows, 128), BF16),
            jax.ShapeDtypeStruct((blocks, 1, 2 * BLK), F32),
            jax.ShapeDtypeStruct((blocks, 128, 2 * BLK), F32),
            jax.ShapeDtypeStruct((4,) + cxs.shape[1:], BF16),
        ],
        compiler_params=params(collective_id=3, has_side_effects=True),
        cost_estimate=cost(1.5e10, 2e7),
        name="attend",
    )(ends, packs, packs, cxs)


def mid_kernel(n, number, capp, attn_ref, cxs_ref, rest_ref, wo_hbm, wr_ref, x_hbm, gain_ref, middle_ref, h_ref, kept_ref, xs_ref, gs_ref, gates_ref, diag_ref, arrived, hs, wo_ref, x_ref, cx, rows_out, grads_out, gates_out, exch_send, exch_recv, hop_send, hop_recv, cross_send, cross_recv, cx_send, cx_recv, fwd_send, fwd_recv, local_sems, load_sems, store_sems):
    tokens, width = x_ref.shape
    split = tokens // 2
    ctx, fsdp = lax.axis_index("ctx"), lax.axis_index("fsdp")
    first = (fsdp * 2 + lax.rem(ctx, 2)) * number
    core, group = neighbours()
    copies = [pltpu.make_async_copy(wo_hbm, wo_ref, local_sems.at[2]), pltpu.make_async_copy(x_hbm, x_ref, local_sems.at[3])]
    for copy in copies:
        copy.start()
    order = (0, 4, 1, 2, 3, 5, 6, 7)

    def load(step):
        refs = (cxs_ref.at[0], cxs_ref.at[1], rest_ref.at[0], diag_ref.at[0], rest_ref.at[1], rest_ref.at[2], rest_ref.at[3], diag_ref.at[1])
        return pltpu.make_async_copy(refs[order[step]], cx.at[step % 2], load_sems.at[step % 2])

    cx_half = cxs_ref.shape[1] // 2

    def cx_cross(i):
        at = pl.ds(i * cx_half, cx_half)
        src = cxs_ref.at[1, at] if i == 0 else rest_ref.at[0, at]
        return send(src, diag_ref.at[0, at], cx_send.at[i], cx_recv.at[i], group[1 - i])

    def cx_core():
        return send(diag_ref.at[0], diag_ref.at[1], cx_send.at[2], cx_recv.at[2], core)

    load(0).start()
    greet([core, group[0]] + [{"ctx": c} for c in others(n)])
    for i in range(2):
        cx_cross(i).start()
    halves = [pl.ds(k * split, split) for k in range(2)]
    exchanges = [(attn_ref.at[:, halves[k]], arrived.at[:, halves[k]], exch_send.at[k], exch_recv.at[k], local_sems.at[4 + k], n) for k in range(2)]
    for exchange in exchanges:
        exchange_start(*exchange)
    for copy in copies:
        copy.wait()

    def hop(i, k):
        return send(hs.at[0, halves[k]], hs.at[(1, 2, 4)[i], halves[k]], hop_send.at[i, k], hop_recv.at[i, k], (group[0], group[1], core)[i])

    def cross(i):
        return send(hs.at[1 + i, halves[i]], hs.at[3, halves[i]], cross_send.at[i], cross_recv.at[i], group[1 - i])

    def forward(i):
        return send(hs.at[1 + i], hs.at[5 + i], fwd_send.at[i], fwd_recv.at[i], core)

    for k in range(2):
        exchange_wait(*exchanges[k])
        at = slice(k * split, (k + 1) * split)
        total = None
        for c in range(n):
            part = dot(arrived[c, at, :], wo_ref[c])
            total = part if total is None else total + part
        middle = x_ref[at, :] + RESIDUAL * total
        middle_ref[at, :] = middle
        normed, _ = norm_parts(middle)
        h = (normed * gain_ref[1:2]).astype(BF16)
        h_ref[at, :] = h
        hs[0, at, :] = h
        for i in range(3):
            hop(i, k).start()
        if k == 0:
            for i in range(2):
                cx_cross(i).wait_recv()
            cx_core().start()
    keep = pltpu.make_async_copy(arrived, kept_ref, local_sems.at[1])
    keep.start()

    def stores(step):
        b = order[step]
        pairs = ((rows_out, xs_ref), (grads_out, gs_ref), (gates_out, gates_ref))
        return [pltpu.make_async_copy(src.at[step % 2], dst.at[:, b], store_sems.at[step % 2, k]) for k, (src, dst) in enumerate(pairs)]

    def place(step):
        b, slot = order[step], step % 2
        load(step).wait()
        if step >= 2:
            for copy in stores(step - 2):
                copy.wait()
        h = hs[b]
        logits = jnp.transpose(dot(h, wr_ref[...]))[:EXPERTS, :]
        raw = jnp.exp(logits - jnp.max(logits, 0, keepdims=True))
        router = raw / jnp.sum(raw, 0, keepdims=True)
        slots = cx[slot, tokens:, :tokens].astype(F32)
        hots = one_hot(slots, first, number, capp)
        places = jnp.concatenate(hots, 0).astype(BF16)
        rows = dot(places, h).astype(BF16)
        grads = dot(places, cx[slot, :tokens, :]).astype(BF16)
        for j in range(number):
            at = slice(j * capp, (j + 1) * capp)
            rows_out[slot, j] = rows[at]
            grads_out[slot, j] = grads[at]
            gate = jnp.sum(hots[j] * own_row(router, first + j), 1, keepdims=True)
            gates_out[slot, j] = jnp.broadcast_to(gate, (capp, 128))
        for copy in stores(step):
            copy.start()
        if step + 2 < 8:
            if step + 2 == 7:
                cx_core().wait_recv()
            load(step + 2).start()

    load(1).start()
    place(0)
    for k in range(2):
        hop(2, k).wait_recv()
    place(1)
    hop(0, 0).wait_recv()
    cross(0).start()
    hop(1, 0).wait_recv()
    hop(1, 1).wait_recv()
    cross(1).start()
    forward(1).start()
    hop(0, 1).wait_recv()
    forward(0).start()
    place(2)
    place(3)
    for i in range(2):
        cross(i).wait_recv()
    forward(2).start()
    place(4)
    for i in range(3):
        forward(i).wait_recv()
        place(5 + i)
    for step in (6, 7):
        for copy in stores(step):
            copy.wait()
    for i in range(2):
        cross(i).wait_send()
        cx_cross(i).wait_send()
    cx_core().wait_send()
    for i in range(3):
        for k in range(2):
            hop(i, k).wait_send()
        forward(i).wait_send()
    keep.wait()


def mid_step(attn, cxs, rest, wo, wr, x, gains, number, capp, n):
    tokens, width = x.shape
    hbm, vmem = pl.BlockSpec(memory_space=pl.ANY), pl.BlockSpec(memory_space=pltpu.VMEM)
    dma = lambda *k: pltpu.SemaphoreType.DMA(k)
    shaped = lambda shape, dtype=BF16: jax.ShapeDtypeStruct(shape, dtype)
    return pl.pallas_call(
        functools.partial(mid_kernel, n, number, capp),
        in_specs=[hbm, hbm, hbm, hbm, vmem, hbm, vmem],
        out_specs=[vmem, vmem, hbm, hbm, hbm, hbm, hbm],
        out_shape=[
            shaped((tokens, width), F32),
            shaped((tokens, width)),
            shaped(attn.shape),
            shaped((number, 8, capp, width)),
            shaped((number, 8, capp, width)),
            shaped((number, 8, capp, 128), F32),
            shaped((2,) + cxs.shape[1:]),
        ],
        scratch_shapes=[
            pltpu.VMEM(attn.shape, BF16),
            pltpu.VMEM((8, tokens, width), BF16),
            pltpu.VMEM(wo.shape, BF16),
            pltpu.VMEM((tokens, width), F32),
            pltpu.VMEM((2,) + cxs.shape[1:], BF16),
            pltpu.VMEM((2, number, capp, width), BF16),
            pltpu.VMEM((2, number, capp, width), BF16),
            pltpu.VMEM((2, number, capp, 128), F32),
            dma(2, n - 1),
            dma(2, n - 1),
            dma(3, 2),
            dma(3, 2),
            dma(2),
            dma(2),
            dma(3),
            dma(3),
            dma(3),
            dma(3),
            dma(6),
            dma(2),
            dma(2, 3),
        ],
        compiler_params=params(collective_id=2, has_side_effects=True),
        cost_estimate=cost(4e9, 5e7),
        name="mid_step",
    )(attn, cxs, rest, wo, wr, x, gains)


RING = 12
LAG_MIDDLE, LAG_ACROSS, LAG_END = 1, 2, 4
ORDER_X, ORDER_Y, ORDER_CORE = 1, 2, 4


class GroupSum:
    def __init__(self, part, rows, lands, own, sems, load, free, first, core, group):
        self.part, self.rows, self.own, self.load, self.free, self.first = part, rows, own, load, free, first
        self.land, self.land_x, self.land_y = lands
        self.core_send, self.core_recv, self.x_send, self.x_recv, self.y_send, self.y_recv = sems
        self.core, self.far, self.near = core, group[0], group[1]

    def place(self, i):
        return self.land.at[i, pl.ds(0, self.rows)]

    def ready(self, which):
        if not self.first:
            pl.semaphore_wait(self.free.at[which], 1)

    def to_core(self, i):
        return send(self.part.at[4 + i], self.place(i), self.core_send.at[i], self.core_recv.at[i], self.core)

    def to_far(self, k):
        return send(self.place(1 + 2 * k), self.land_x.at[k, pl.ds(0, self.rows)], self.x_send.at[k], self.x_recv.at[k], self.far)

    def to_near(self):
        return send(self.place(2), self.land_y.at[pl.ds(0, self.rows)], self.y_send.at[0], self.y_recv.at[0], self.near)

    def fetch(self, i):
        return pltpu.make_async_copy(self.part.at[i], self.own.at[i % 2, pl.ds(0, self.rows)], self.load.at[i % 2])

    def start(self):
        self.ready(0)
        for i in (1, 3, 2, 0):
            self.to_core(i).start()

    def over_cores(self):
        order = (1, 3, 2, 0)
        if self.own is not None:
            self.fetch(1).start()
        for step, i in enumerate(order):
            if self.own is None:
                mine = self.part[i]
            else:
                self.fetch(i).wait()
                mine = self.own[i % 2, : self.rows]
            self.to_core(i).wait_recv()
            self.land[i, : self.rows] = (self.land[i, : self.rows].astype(F32) + mine.astype(F32)).astype(BF16)
            if self.own is not None and step < 3:
                self.fetch(order[step + 1]).start()
            if i % 2 == 1:
                if step == 0:
                    self.ready(1)
                self.to_far(i // 2).start()

    def over_x(self, between=None):
        for k in (1, 0):
            if k == 0 and between is not None:
                between()
            self.to_far(k).wait_recv()
            both = self.land[2 * k, : self.rows].astype(F32) + self.land_x[k, : self.rows].astype(F32)
            self.land[2 * k, : self.rows] = both.astype(BF16)
            if k == 1:
                self.ready(2)
                self.to_near().start()

    def finish(self):
        self.to_near().wait_recv()
        for i in range(4):
            self.to_core(i).wait_send()
        for k in range(2):
            self.to_far(k).wait_send()
        self.to_near().wait_send()
        return self.land[0, : self.rows].astype(F32) + self.land_y[: self.rows].astype(F32)

    def release(self):
        for which, device in enumerate((self.core, self.far, self.near)):
            pl.semaphore_signal(self.free.at[which], inc=1, device_id=device, device_id_type=MESH)


class LineSum:
    def __init__(self, count, own_ref, other_ref, inbox, across, mine, sems):
        self.count, self.own_ref, self.other_ref = count, own_ref, other_ref
        self.inbox, self.across, self.mine = inbox, across, mine
        self.line_send, self.line_recv, self.mid_send, self.mid_recv, self.side_send, self.side_recv, self.store, self.load = sems
        ctx = lax.axis_index("ctx")
        z = ctx // 2
        self.middle = (z == 1) | (z == 2)
        self.line = {"ctx": jnp.where(z % 2 == 0, ctx + 2, ctx - 2)}
        self.peer = {"ctx": jnp.where(z == 1, ctx + 2, ctx - 2)}
        self.side = {"ctx": flip(ctx, 1)}

    def send_line(self, src, i):
        s = lax.rem(i, RING)
        return send(src, self.inbox.at[s], self.line_send.at[s], self.line_recv.at[s], self.line)

    def send_mid(self, i):
        s = lax.rem(i, RING)
        return send(self.inbox.at[s], self.across.at[s], self.mid_send.at[s], self.mid_recv.at[s], self.peer)

    def send_side(self, src, i):
        return send(src, self.other_ref.at[i], self.side_send.at[lax.rem(i, RING)], self.side_recv.at[i], self.side)

    def keep(self, src, i):
        return pltpu.make_async_copy(src, self.own_ref.at[i], self.store.at[lax.rem(i, RING)])

    def fetch(self, src, i):
        s = lax.rem(i, 4)
        return pltpu.make_async_copy(src, self.mine.at[s], self.load.at[s])

    def drain_middle(self, i):
        src = self.across.at[lax.rem(i, RING)]
        self.send_line(src, i).wait_send()
        self.send_side(src, i).wait_send()
        self.keep(src, i).wait()

    def drain_end(self, i):
        src = self.inbox.at[lax.rem(i, RING)]
        self.send_side(src, i).wait_send()
        self.keep(src, i).wait()

    def tick(self, t, source):
        count = self.count
        fixed = isinstance(t, int)

        def when(condition):
            if fixed:
                return (lambda f: f()) if condition else (lambda f: None)
            return pl.when(condition)

        i32 = (lambda v: jnp.int32(v)) if fixed else (lambda v: v)

        @pl.when(self.middle)
        def _():
            @when((t >= LAG_MIDDLE) & (t < count + LAG_MIDDLE))
            def _():
                i = i32(t - LAG_MIDDLE)

                @when(t >= LAG_ACROSS + 4)
                def _():
                    self.drain_middle(i32(t - LAG_ACROSS - 4))

                s = lax.rem(i, RING)
                self.fetch(self.own_ref.at[i], i).wait()
                self.send_line(self.inbox.at[s], i).wait_recv()
                self.inbox[s] = self.inbox[s] + self.mine[lax.rem(i, 4)]
                self.send_mid(i).start()

            @when(t < count)
            def _():
                self.fetch(source(t), i32(t)).start()

            @when((t >= LAG_ACROSS) & (t < count + LAG_ACROSS))
            def _():
                i = i32(t - LAG_ACROSS)
                s = lax.rem(i, RING)
                self.send_mid(i).wait()
                self.across[s] = self.across[s] + self.inbox[s]
                self.send_line(self.across.at[s], i).start()
                self.send_side(self.across.at[s], i).start()
                self.keep(self.across.at[s], i).start()

        @pl.when(jnp.logical_not(self.middle))
        def _():
            @when(t < count)
            def _():
                @when(t >= LAG_END + 2)
                def _():
                    self.drain_end(i32(t - LAG_END - 2))

                @when(t >= 3)
                def _():
                    self.send_line(self.mine.at[0], i32(t - 3)).wait_send()

                self.send_line(source(t), i32(t)).start()

            @when(t >= LAG_END)
            def _():
                i = i32(t - LAG_END)
                s = lax.rem(i, RING)
                self.send_line(self.inbox.at[s], i).wait_recv()
                self.send_side(self.inbox.at[s], i).start()
                self.keep(self.inbox.at[s], i).start()

    def finish(self):
        count = self.count

        @pl.when(self.middle)
        def _():
            for i in range(count + LAG_MIDDLE - LAG_ACROSS - 4, count):
                self.drain_middle(jnp.int32(i))

        @pl.when(jnp.logical_not(self.middle))
        def _():
            for i in range(count - 3, count):
                self.send_line(self.mine.at[0], jnp.int32(i)).wait_send()
            for i in range(count - LAG_END - 2, count):
                self.drain_end(jnp.int32(i))

        def arrived(i, carry):
            self.send_side(self.mine.at[0], i).wait_recv()
            return carry

        lax.fori_loop(0, count, arrived, 0)


def backward_kernel(
    n,
    length,
    capp,
    ends_ref,
    xs_ref,
    gs_ref,
    gates_ref,
    wg_ref,
    wu_ref,
    wd_ref,
    cxs_ref,
    rest_ref,
    diag_ref,
    full_ref,
    weights_ref,
    packs_hbm,
    table_hbm,
    cot_hbm,
    wo_hbm,
    attn_hbm,
    x_hbm,
    h_attn_hbm,
    h_ref,
    middle_ref,
    wr_ref,
    gains_ref,
    lse_ref,
    own_ref,
    other_ref,
    pieces_ref,
    outs_ref,
    backs_ref,
    gx_ref,
    yp_ref,
    grad_x_ref,
    mixed_ref,
    inbox,
    across,
    mine,
    land,
    land_x,
    land_y,
    y_land,
    y_land_x,
    y_land_y,
    own_buf,
    late_pieces,
    ga_in,
    grads_in,
    line_send,
    line_recv,
    mid_send,
    mid_recv,
    side_send,
    side_recv,
    line_store,
    line_load,
    ga_send,
    ga_recv,
    gr_send,
    gr_recv,
    group_sems,
    group_load,
    free,
    local_sems,
    full_sems,
    w_sems,
    load_sems,
    store_sems,
    comb_sems,
    part_sems,
):
    tokens, width = h_ref.shape
    half = length // 2
    rows = tokens // 2
    shard = width // 4
    blocks = length // BLK
    number = xs_ref.shape[0]
    ff = wg_ref.shape[2]
    ctx, fsdp = lax.axis_index("ctx"), lax.axis_index("fsdp")
    side = lax.rem(ctx, 2)
    first = (fsdp * 2 + side) * number
    core, group = neighbours()
    sub = own_ref.shape[1]
    cuts = PIECE // sub
    early = number * 6 * cuts
    line = LineSum(early + 2 * cuts, own_ref, other_ref, inbox, across, mine, (line_send, line_recv, mid_send, mid_recv, side_send, side_recv, line_store, line_load))

    def source(t):
        return pieces_ref.at[t // cuts, pl.ds(pl.multiple_of(lax.rem(t, cuts) * sub, sub), sub)]

    def tick(t):
        line.tick(jnp.int32(t) if isinstance(t, int) else t, source)

    sems = lambda k: [group_sems.at[k, j] for j in range(6)]
    lands = (land, land_x, land_y)
    ext = tokens + EXPERTS
    gx = GroupSum(gx_ref, 2 * ext, lands, None, sems(0), None, free, True, core, group)
    ys = GroupSum(yp_ref, 2 * tokens, (y_land, y_land_x, y_land_y), own_buf, sems(1), group_load, free, True, core, group)

    def strip(r):
        f = fsdp
        if r & ORDER_X:
            f = flip(f, 2)
        if r & ORDER_CORE:
            f = flip(f, 1)
        return 2 * f + (1 - side if r & ORDER_Y else side)

    def experts(wg, wu, wd, xb, gb, gateb, stage, out_acc, back_acc, outb, backb, go, dgate, comb_o, comb_b, gst, yst, slots):
        def loads(e):
            s = lax.rem(e, 2)
            at = side * number + e
            pairs = ((wg_ref.at[at], wg), (wu_ref.at[at], wu), (wd_ref.at[at], wd), (xs_ref.at[e], xb), (gs_ref.at[e], gb), (gates_ref.at[e], gateb))
            return [pltpu.make_async_copy(src, dst.at[s], load_sems.at[s, k]) for k, (src, dst) in enumerate(pairs)]

        def slot_copy(b):
            refs = (cxs_ref.at[0], cxs_ref.at[1], rest_ref.at[0], diag_ref.at[0], rest_ref.at[1], rest_ref.at[2], rest_ref.at[3], diag_ref.at[1])
            return pltpu.make_async_copy(refs[b].at[pl.ds(tokens, EXPERTS), pl.ds(0, tokens)], slots.at[b], part_sems.at[0, b])

        def stores(e):
            pairs = (
                (stage.at[pl.ds(0, 3)], pieces_ref.at[pl.ds(6 * e, 3)]),
                (stage.at[pl.ds(3, 3)], pieces_ref.at[pl.ds(6 * e + 3, 3)]),
                (outb, outs_ref.at[e]),
                (backb, backs_ref.at[e]),
            )
            return [pltpu.make_async_copy(src, dst, store_sems.at[k]) for k, (src, dst) in enumerate(pairs)]

        for copy in loads(jnp.int32(0)):
            copy.start()
        for b in range(8):
            slot_copy(b).start()
        greet([core, group[0]] + [{"ctx": c} for c in others(n)])

        def one(e, carry):
            s = lax.rem(e, 2)

            @pl.when(e + 1 < number)
            def _():
                for copy in loads(e + 1):
                    copy.start()

            for copy in loads(e):
                copy.wait()

            @pl.when(e > 0)
            def _():
                for copy in stores(e - 1)[2:]:
                    copy.wait()

            x = xb[s]
            gate = gateb[s][:, :1]
            go[...] = (gate * (RESIDUAL * gb[s].astype(F32))).astype(BF16)
            part = ff // 2
            for chunk in range(2):
                at = slice(chunk * part, (chunk + 1) * part)
                wgc, wuc, wdc = wg[s, :, at], wu[s, :, at], wd[s, at, :]
                pre_gate = dot(x, wgc)
                pre_up = dot(x, wuc)
                sig = jax.nn.sigmoid(pre_gate)
                hidden = (pre_gate * sig * pre_up).astype(BF16)
                out_part = dot(hidden, wdc)
                grad_hidden = dot(go[...], wdc, NT)
                grad_gate = (grad_hidden * pre_up * sig * (1.0 + pre_gate * (1.0 - sig))).astype(BF16)
                grad_up = (grad_hidden * pre_gate * sig).astype(BF16)
                row_part = dot(grad_gate, wgc, NT) + dot(grad_up, wuc, NT)
                dwg = dot(x, grad_gate, TN).astype(BF16)
                dwu = dot(x, grad_up, TN).astype(BF16)
                dwd = dot(hidden, go[...], TN).astype(BF16)
                for k in range(2):
                    cut = slice(k * PIECE, (k + 1) * PIECE)
                    stage[3 * chunk + k, :, :part] = dwg[cut]
                    stage[3 * chunk + k, :, part:] = dwu[cut]
                    stage[3 * chunk + 2, k * part : (k + 1) * part, :] = dwd[:, cut]
                stores(e)[chunk].start()
                if chunk == 0:
                    out_acc[...] = out_part
                    back_acc[...] = row_part
                    stores(e)[0].wait()
                    tick(2 * e)
                else:
                    out = (out_acc[...] + out_part).astype(BF16).astype(F32)
                    outb[...] = (gate * out).astype(BF16)
                    backb[...] = (back_acc[...] + row_part).astype(BF16)
                    grad = jnp.sum(RESIDUAL * gb[s].astype(F32) * out, 1, keepdims=True)
                    dgate[e] = jnp.broadcast_to(grad, dgate.shape[1:])
            for copy in stores(e)[2:]:
                copy.start()
            stores(e)[1].wait()
            tick(2 * e + 1)
            return carry

        lax.fori_loop(0, number, one, 0)
        for copy in stores(jnp.int32(number - 1))[2:]:
            copy.wait()
        for b in range(8):
            slot_copy(b).wait()

        def which(s):
            k = lax.rem(s, 4)
            i = jnp.where(k == 0, 1, jnp.where(k == 1, 3, jnp.where(k == 2, 2, 0)))
            return jnp.where(s < 4, 4 + i, i), i

        def comb(s):
            k = lax.rem(s, 2)
            at = pl.ds(pl.multiple_of(which(s)[0] * capp, 16), capp)
            return [
                pltpu.make_async_copy(outs_ref.at[:, at], comb_o.at[k], comb_sems.at[0, k]),
                pltpu.make_async_copy(backs_ref.at[:, at], comb_b.at[k], comb_sems.at[1, k]),
            ]

        def put(s):
            k = lax.rem(s, 2)
            r, _ = which(s)
            return [
                pltpu.make_async_copy(gst.at[k], gx_ref.at[r], part_sems.at[1, k]),
                pltpu.make_async_copy(yst.at[k], yp_ref.at[r], part_sems.at[1, 2 + k]),
            ]

        for copy in comb(jnp.int32(0)):
            copy.start()

        def join(s, carry):
            k = lax.rem(s, 2)
            r, i = which(s)

            @pl.when(s + 1 < 8)
            def _():
                for copy in comb(s + 1):
                    copy.start()

            for copy in comb(s):
                copy.wait()

            @pl.when(s >= 2)
            def _():
                put(s - 2)[1].wait()

            hots = one_hot(slots[r].astype(F32), first, number, capp)
            places = jnp.concatenate(hots, 0).astype(BF16)
            y = dot(places, comb_o[k].reshape(number * capp, width), TN).astype(BF16)
            back = dot(places, comb_b[k].reshape(number * capp, width), TN).astype(BF16)
            extra = jnp.zeros((EXPERTS, 2 * tokens), F32)
            for j in range(number):
                grads = dgate[j, pl.ds(pl.multiple_of(r * capp, 16), capp), :][:, :1]
                grad = jnp.sum(hots[j] * grads, 0, keepdims=True)
                high = grad.astype(BF16).astype(F32)
                extra = jnp.where(row_iota(extra.shape) == first + j, jnp.concatenate([high, grad - high], 1), extra)
            for q in range(2):
                yst[k, q * tokens : (q + 1) * tokens, :] = y[:, q * PIECE : (q + 1) * PIECE]
                gst[k, q * ext : q * ext + tokens, :] = back[:, q * PIECE : (q + 1) * PIECE]
            gst[k, tokens:ext, :] = extra.astype(BF16)
            gst[k, ext + tokens :, :] = jnp.zeros((EXPERTS, PIECE), BF16)
            put(s)[1].start()

            @pl.when(s < 4)
            def _():
                put(s)[0].start()
                put(s)[0].wait()
                gx.to_core(i).start()

            @pl.when(s >= 4)
            def _():
                gx.to_core(i).wait_recv()
                land[i, : gx.rows] = (land[i, : gx.rows].astype(F32) + gst[k].astype(F32)).astype(BF16)

            @pl.when((s == 4) | (s == 5))
            def _():
                gx.to_far(s - 4).start()

            @pl.when(lax.rem(s, 2) == 1)
            def _():
                tick(2 * number + s // 2)

            return carry

        lax.fori_loop(0, 8, join, 0)
        for s in range(6, 8):
            put(jnp.int32(s))[1].wait()

    slots_rows = xs_ref.shape[1]
    pl.run_scoped(
        experts,
        pltpu.VMEM((2, width, ff), BF16),
        pltpu.VMEM((2, width, ff), BF16),
        pltpu.VMEM((2, ff, width), BF16),
        pltpu.VMEM((2, slots_rows, width), BF16),
        pltpu.VMEM((2, slots_rows, width), BF16),
        pltpu.VMEM((2, slots_rows, 128), F32),
        pltpu.VMEM((6, PIECE, PIECE), BF16),
        pltpu.VMEM((slots_rows, width), F32),
        pltpu.VMEM((slots_rows, width), F32),
        pltpu.VMEM((slots_rows, width), BF16),
        pltpu.VMEM((slots_rows, width), BF16),
        pltpu.VMEM((slots_rows, width), BF16),
        pltpu.VMEM((number, slots_rows, 128), F32),
        pltpu.VMEM((2, number, capp, width), BF16),
        pltpu.VMEM((2, number, capp, width), BF16),
        pltpu.VMEM((2, 2 * ext, PIECE), BF16),
        pltpu.VMEM((2, 2 * tokens, PIECE), BF16),
        pltpu.VMEM((8, EXPERTS, tokens), BF16),
    )
    at_tick = [2 * number + 4]

    def go_on(k=1):
        for _ in range(k):
            tick(at_tick[0])
            at_tick[0] += 1

    def backward(packs, table, keys, values, keys_t, grad_q, grad_k, grad_v, acc, full_buf, ga, pack_out, wbuf, total, grad_middle, dgain, col, small, columns, cot, wo, attn, x_in, h_attn):
        ws = GroupSum(small, PIECE, lands, None, sems(2), None, free, False, core, group)
        cs = GroupSum(columns, PIECE + 16, lands, None, sems(3), None, free, False, core, group)
        copies = [
            pltpu.make_async_copy(src, dst, local_sems.at[4 + k])
            for k, (src, dst) in enumerate(
                ((cot_hbm, cot), (wo_hbm, wo), (attn_hbm, attn), (packs_hbm, packs), (table_hbm, table), (x_hbm, x_in), (h_attn_hbm, h_attn))
            )
        ]
        for copy in copies:
            copy.start()
        small[:, PIECE // 2 : PIECE, :] = jnp.zeros((8, PIECE // 2, PIECE), BF16)
        columns[:, PIECE:, :] = jnp.zeros((8, 16, PIECE), BF16)
        go_on(2)
        gx.over_x(go_on)
        go_on(2)
        arrived = gx.finish()
        arrived = jnp.concatenate([arrived[:ext], arrived[ext:]], 1)
        gx.release()

        h = h_ref[...]
        gain = gains_ref[1:2]
        extra = arrived[tokens:, :]
        grad_router = extra[:, :tokens] + extra[:, tokens : 2 * tokens]
        grad_router = jnp.transpose(jnp.concatenate([grad_router, jnp.zeros((128 - EXPERTS, tokens), F32)], 0))
        logits = dot(h, wr_ref[...])
        logits = jnp.where(lane_iota(logits.shape) < EXPERTS, logits, MASKED)
        raw = jnp.exp(logits - jnp.max(logits, -1, keepdims=True))
        router = raw / jnp.sum(raw, -1, keepdims=True)
        grad_logits = (router * (grad_router - jnp.sum(router * grad_router, -1, keepdims=True))).astype(BF16)
        go_on()
        grad_h = arrived[:tokens, :] + dot(grad_logits, wr_ref[...], NT)
        normed, scale = norm_parts(middle_ref[...])
        dgain[1:2, :] = jnp.sum(grad_h * normed, 0, keepdims=True)
        for copy in copies[:3]:
            copy.wait()
        grad_mid = cot[...] + norm_back(grad_h * gain, normed, scale)
        grad_middle[...] = grad_mid
        grad_branch = (RESIDUAL * grad_mid).astype(BF16)
        for c in range(n):
            ga[c] = dot(grad_branch, wo[c], NT).astype(BF16)
        ga_exchange = (ga, ga_in, ga_send, ga_recv, local_sems.at[2], n)
        exchange_start(*ga_exchange)
        go_on()
        col[:, :128] = dot(h, grad_logits, TN).astype(BF16)
        for r in range(8):
            at = strip(r)
            dwo = dot(attn[at], grad_branch, TN).astype(BF16)
            small[r, 0:128, :] = dwo[:, :PIECE]
            small[r, 128:256, :] = dwo[:, PIECE:]
            small[r, 256:384, 0:128] = col[pl.ds(pl.multiple_of(at * 128, 128), 128), 0:128]
        ws.start()
        ys.start()
        go_on()
        copies[3].wait()
        for hh in range(2):
            for c in range(n):
                kk, vv = pair_keys(packs[c, hh, :, 128:256].astype(F32))
                at = hh * half + c * rows
                keys[at : at + rows, :] = kk.astype(BF16)
                values[at : at + rows, :] = vv.astype(BF16)
                keys_t[:, at : at + rows] = jnp.transpose(kk).astype(BF16)
        grad_k[...] = jnp.zeros_like(grad_k)
        grad_v[...] = jnp.zeros_like(grad_v)
        go_on()
        ws.over_cores()
        ys.over_cores()
        go_on()
        exchange_wait(*ga_exchange)

        per = BLK // rows
        per_half = blocks // 2

        def fetch_full(b):
            return pltpu.make_async_copy(full_ref.at[b], full_buf.at[lax.rem(b, 2)], full_sems.at[lax.rem(b, 2)])

        fetch_full(jnp.int32(0)).start()
        attend_tick = at_tick[0]

        def attend(block, carry):
            late = block // per_half
            c0 = lax.rem(block, per_half) * per
            q2 = jnp.concatenate([packs[c0 + k, late, :, :128] for k in range(per)], 0)
            q2 = stack_heads((q2.astype(F32) * ATTN_SCALE).astype(BF16))
            g2 = stack_heads(jnp.concatenate([ga_in[c0 + k, pl.ds(pl.multiple_of(late * rows, rows), rows), :] for k in range(per)], 0))
            position, start = query_rows(ends_ref, block, length)
            lse = lse_ref[block]
            shift = jnp.where(start > 0, MASKED, 0.0) - lse

            @pl.when(block + 1 < blocks)
            def _():
                fetch_full(block + 1).start()

            fetch_full(block).wait()
            delta = jnp.sum(jnp.transpose(g2.astype(F32)) * full_buf[lax.rem(block, 2)], 0, keepdims=True)
            acc[...] = jnp.zeros_like(acc)

            def body(kb, whole, carry):
                at = pl.multiple_of(kb * BLK, BLK)
                scores = dot(keys[pl.ds(at, BLK), :], q2, NT)
                if whole:
                    probs = jnp.exp(scores + shift)
                else:
                    where = key_position(kb, length)
                    probs = jnp.where((where <= position) & (where >= start), jnp.exp(scores - lse), 0.0)
                grad_probs = dot(values[pl.ds(at, BLK), :], g2, NT)
                grad_scores = (probs * (grad_probs - delta)).astype(BF16)
                acc[...] += dot(keys_t[:, pl.ds(at, BLK)], grad_scores)
                grad_k[pl.ds(at, BLK), :] += dot(grad_scores, q2)
                grad_v[pl.ds(at, BLK), :] += dot(probs.astype(BF16), g2)

                if not whole:

                    @pl.when((kb == block) & ((block == per_half) | (block == per_half + 1)))
                    def _():
                        tick(attend_tick + 2 + 2 * (block - per_half))

                return carry

            block_loop(block, per_half, body, 0)
            grad_q[pl.ds(pl.multiple_of(block * BLK, BLK), BLK), :] = fold_heads(jnp.transpose(acc[...]))

            @pl.when((block == 1) | (block >= 3))
            def _():
                past = block - per_half
                late_tick = jnp.where(past < 2, 3 + 2 * past, 4 + past)
                tick(attend_tick + jnp.where(block < per_half, block // 2, late_tick))

            return carry

        lax.fori_loop(0, blocks, attend, 0)
        at_tick[0] += blocks
        copies[4].wait()
        for c in range(n):
            for hh in range(2):
                at = slice(hh * half + c * rows, hh * half + (c + 1) * rows)
                kk = grad_k[at, :]
                vv = grad_v[at, :]
                kk = kk + pltpu.roll(kk, 64, 1)
                vv = vv + pltpu.roll(vv, 64, 1)
                both = jnp.where(lane_iota(kk.shape) < 64, kk, vv)
                package = jnp.concatenate([grad_q[at, :] * ATTN_SCALE, both], -1)
                pack_out[c, hh * rows : (hh + 1) * rows, :] = turn(package, table[at, :], -1.0).astype(BF16)
        gr_exchange = (pack_out, grads_in, gr_send, gr_recv, local_sems.at[3], n)
        exchange_start(*gr_exchange)

        def fetch_w(c):
            slot = lax.rem(c, 2)
            at = pl.ds(pl.multiple_of(c * 128, 128), 128)
            return [
                pltpu.make_async_copy(weights_ref.at[1 - k, :, :, at], wbuf.at[slot, :, :, pl.ds(128 * k, 128)], w_sems.at[slot, k])
                for k in range(2)
            ]

        for copy in fetch_w(jnp.int32(0)):
            copy.start()
        go_on()
        ws.over_x()
        ys.over_x()
        go_on(2)
        total[...] = jnp.zeros_like(total)
        late_pieces[:PIECE] = ws.finish().astype(BF16)
        ws.release()
        ffn = ys.finish()
        mixed_ref[...] = middle_ref[...] + RESIDUAL * jnp.concatenate([ffn[:tokens], ffn[tokens:]], 1)
        go_on(3)
        exchange_wait(*gr_exchange)
        copies[5].wait()
        copies[6].wait()

        columns_tick = at_tick[0]

        def finish_columns(c, carry):
            @pl.when(c + 1 < n)
            def _():
                for copy in fetch_w(c + 1):
                    copy.start()

            for copy in fetch_w(c):
                copy.wait()
            slot = lax.rem(c, 2)
            g = grads_in[c]
            col[...] = dot(h_attn[...], g, TN).astype(BF16)
            for r in range(8):
                at = pl.ds(pl.multiple_of(strip(r) * 128, 128), 128)
                columns[r, pl.ds(pl.multiple_of(c // 2 * 128, 128), 128), pl.ds(pl.multiple_of(lax.rem(c, 2) * PACK, PACK), PACK)] = col[at, :]
            for f in range(4):
                total[:, f * shard : (f + 1) * shard] += dot(g, wbuf[slot, f, :shard, :], NT)

            @pl.when(lax.rem(c, 4) == 3)
            def _():
                tick(columns_tick + c // 4)

            return carry

        lax.fori_loop(0, n, finish_columns, 0)
        at_tick[0] += n // 4
        normed, scale = norm_parts(x_in[...])
        grad_h = total[...]
        dgain[0:1, :] = jnp.sum(grad_h * normed, 0, keepdims=True)
        grad_x_ref[...] = grad_middle[...] + norm_back(grad_h * gains_ref[0:1], normed, scale)
        for r in range(8):
            at = pl.ds(pl.multiple_of(strip(r) * 128, 128), 128)
            row = row_iota((16, 128))
            both = jnp.where(row == 0, dgain[0:1, at], jnp.where(row == 1, dgain[1:2, at], 0.0))
            columns[r, PIECE:, 0:128] = both.astype(BF16)
        cs.start()
        go_on()
        cs.over_cores()
        go_on(3)
        cs.over_x(go_on)
        go_on(3)
        summed = cs.finish().astype(BF16)
        late_pieces[PIECE:] = summed[:PIECE]
        late_pieces[384:400] = summed[PIECE:]

    f32, bf = (lambda *shape: pltpu.VMEM(shape, F32)), (lambda *shape: pltpu.VMEM(shape, BF16))
    pl.run_scoped(
        backward,
        bf(*packs_hbm.shape),
        f32(*table_hbm.shape),
        bf(length, 128),
        bf(length, 128),
        bf(128, length),
        f32(length, 128),
        f32(length, 128),
        f32(length, 128),
        f32(128, 2 * BLK),
        f32(2, 128, 2 * BLK),
        bf(n, tokens, 128),
        bf(n, tokens, PACK),
        bf(2, 4, weights_ref.shape[2], PACK),
        f32(tokens, width),
        f32(tokens, width),
        f32(8, width),
        bf(width, PACK),
        bf(8, PIECE, PIECE),
        bf(8, PIECE + 16, PIECE),
        f32(tokens, width),
        bf(*wo_hbm.shape),
        bf(*attn_hbm.shape),
        f32(tokens, width),
        bf(tokens, width),
    )

    def rest(t, carry):
        tick(t)
        return carry

    lax.fori_loop(at_tick[0], early, rest, 0)

    def late_source(t):
        return late_pieces.at[pl.ds(pl.multiple_of((t - early) * sub, sub), sub)]

    def late(t, carry):
        line.tick(t, late_source)
        return carry

    lax.fori_loop(early, line.count + LAG_END, late, 0)
    line.finish()


def backward_step(ends, xs, gs, gates, w_gate, w_up, w_down, cxs, rest, diag, full, weights, packs, table, cot, wo, attn, x, h_attn, h, middle, wr, gains, lse, n, length, capp):
    tokens, width = x.shape
    number, slots_rows, _ = xs.shape
    hbm, vmem = pl.BlockSpec(memory_space=pl.ANY), pl.BlockSpec(memory_space=pltpu.VMEM)
    smem = pl.BlockSpec(memory_space=pltpu.SMEM)
    dma = lambda *k: pltpu.SemaphoreType.DMA(k)
    shaped = lambda shape, dtype=BF16: jax.ShapeDtypeStruct(shape, dtype)
    sub = PIECE // 2
    piece = (sub, PIECE)
    count = (number * 6 + 2) * 2
    land_rows = max(2 * (tokens + EXPERTS), PIECE + 16)
    return pl.pallas_call(
        functools.partial(backward_kernel, n, length, capp),
        in_specs=[smem] + [hbm] * 18 + [vmem] * 5,
        out_specs=[hbm] * 7 + [vmem, vmem],
        out_shape=[
            shaped((count,) + piece),
            shaped((count,) + piece),
            shaped((number * 6, PIECE, PIECE)),
            shaped(xs.shape),
            shaped(xs.shape),
            shaped((8, 2 * (tokens + EXPERTS), PIECE)),
            shaped((8, 2 * tokens, PIECE)),
            shaped((tokens, width), F32),
            shaped((tokens, width), F32),
        ],
        scratch_shapes=[
            pltpu.VMEM((RING,) + piece, BF16),
            pltpu.VMEM((RING,) + piece, BF16),
            pltpu.VMEM((4,) + piece, BF16),
            pltpu.VMEM((4, land_rows, PIECE), BF16),
            pltpu.VMEM((2, land_rows, PIECE), BF16),
            pltpu.VMEM((land_rows, PIECE), BF16),
            pltpu.VMEM((4, 2 * tokens, PIECE), BF16),
            pltpu.VMEM((2, 2 * tokens, PIECE), BF16),
            pltpu.VMEM((2 * tokens, PIECE), BF16),
            pltpu.VMEM((2, 2 * tokens, PIECE), BF16),
            pltpu.VMEM((2 * PIECE, PIECE), BF16),
            pltpu.VMEM((n, tokens, 128), BF16),
            pltpu.VMEM((n, tokens, PACK), BF16),
            dma(RING),
            dma(RING),
            dma(RING),
            dma(RING),
            dma(RING),
            dma(count),
            dma(RING),
            dma(4),
            dma(n - 1),
            dma(n - 1),
            dma(n - 1),
            dma(n - 1),
            dma(4, 6, 4),
            dma(2),
            pltpu.SemaphoreType.REGULAR((3,)),
            dma(11),
            dma(2),
            dma(2, 2),
            dma(2, 6),
            dma(4),
            dma(2, 2),
            dma(2, 8),
        ],
        compiler_params=params(63, collective_id=0, has_side_effects=True),
        cost_estimate=cost(6e10, 1e9),
        name="backward_step",
    )(ends, xs, gs, gates, w_gate, w_up, w_down, cxs, rest, diag, full, weights, packs, table, cot, wo, attn, x, h_attn, h, middle, wr, gains, lse)


def local(
    inputs,
    cotangent,
    doc_lengths,
    routes,
    attn_gain,
    ffn_gain,
    w_query,
    key_weight,
    value_weight,
    w_out,
    w_router,
    w_gate,
    w_up,
    w_down,
):
    rows = inputs.shape[2]
    width = inputs.shape[3]
    n = lax.axis_size("ctx")
    fsdp = lax.axis_size("fsdp")
    me, mine = lax.axis_index("ctx"), lax.axis_index("fsdp")
    tokens = 2 * rows
    length = tokens * n
    experts_here = w_gate.shape[0]
    number = experts_here // 2
    capacity = 5 * tokens * TOP // (4 * EXPERTS)
    capp = -(-capacity // 16) * 16
    shard = width // fsdp
    heads = QUERY_HEADS // n
    head_lanes = heads * HEAD_DIMENSION
    copies = n // KEY_VALUE_HEADS
    bits = group_bits(fsdp)

    x = inputs.reshape(tokens, width)
    cot = cotangent.reshape(tokens, width)
    side = me % 2
    base = (side * number).astype(jnp.int32).reshape(1)
    first = (mine * experts_here + side * number).astype(jnp.int32).reshape(1)
    index = jnp.stack([side * number, (1 - side) * number]).astype(jnp.int32)
    ends = doc_lengths
    table = jnp.asarray(rotary_table(length))

    out_part = w_out.reshape(shard // head_lanes, head_lanes, width)
    if head_lanes < 128:
        out_part = jnp.pad(out_part, ((0, 0), (0, 128 - head_lanes), (0, 0)))
    merge = lambda a: a.reshape(number, -1, a.shape[-1])

    if n == 8 and fsdp == 4:
        packs, h_attn, weights, wo, wr, cxs, gains = front(
            w_query,
            key_weight,
            value_weight,
            out_part,
            jnp.transpose(w_router),
            jnp.stack([attn_gain, ffn_gain]),
            x,
            table.reshape(2, n, rows, 256),
            jnp.transpose(routes[0], (0, 2, 1)),
            cot,
            capacity,
            n,
        )
        wo, wr = wo.reshape(n, 128, width), wr.reshape(width, 128)
        packs = packs.reshape(n, 2, rows, PACK)
        attn, lse, full, cx_rest = attend(ends, packs, cxs, length)
        middle, h_ffn, attn, xs, gs, gates, diag = mid_step(attn.reshape(n, tokens, 128), cxs, cx_rest, wo, wr, x, gains, number, capp, n)
        own, other, _, _, _, _, _, grad_x, mixed = backward_step(
            ends,
            merge(xs),
            merge(gs),
            merge(gates),
            w_gate,
            w_up,
            w_down,
            cxs,
            cx_rest,
            diag,
            full,
            weights,
            packs,
            table,
            cot,
            wo,
            attn,
            x,
            h_attn,
            h_ffn,
            middle,
            wr,
            gains,
            lse,
            n,
            length,
            capp,
        )
        own, other = own.reshape(-1, PIECE, PIECE), other.reshape(-1, PIECE, PIECE)
        shapes = [w.shape for w in (w_gate, w_up, w_down)]
        outs = tail(index, own, other, mixed, grad_x, shapes, shard)
        return (
            outs[3].reshape(inputs.shape),
            outs[4].reshape(inputs.shape),
            outs[10].reshape(shard),
            outs[11].reshape(shard),
            outs[5],
            outs[6],
            outs[7],
            outs[8],
            jnp.transpose(outs[9]),
            outs[0],
            outs[1],
            outs[2],
        )

    else:
        own_table = lax.dynamic_slice_in_dim(table.reshape(2, n, rows, 256), me, 1, 1).reshape(tokens, 256)
        query_part = w_query.reshape(shard, n, head_lanes)
        if head_lanes < 128:
            query_part = jnp.pad(query_part, ((0, 0), (0, 0), (0, 128 - head_lanes)))
        key_part = jnp.repeat(key_weight.reshape(shard, KEY_VALUE_HEADS, HEAD_DIMENSION), copies, 1)
        value_part = jnp.repeat(value_weight.reshape(shard, KEY_VALUE_HEADS, HEAD_DIMENSION), copies, 1)
        packed = jnp.concatenate([query_part, key_part, value_part], -1).reshape(shard, n * PACK)
        padding = 2 * 16 * (shard // 32 + 1) - shard
        gains = jnp.pad(jnp.stack([attn_gain, ffn_gain]), ((0, padding - 2), (0, n * PACK - shard)))
        packed = jnp.concatenate([packed, gains], 0)
        router_part = jnp.pad(w_router, ((0, 0), (0, 128 - EXPERTS)))
        weights = lax.all_gather(packed, "fsdp", axis=0)
        gain_one = weights[:, shard, :shard].reshape(1, width).astype(F32)
        gain_two = weights[:, shard + 1, :shard].reshape(1, width).astype(F32)
        wo = lax.all_gather(out_part, "fsdp", axis=0, tiled=True)
        wr = lax.all_gather(router_part, "fsdp", axis=0, tiled=True)
        cxs = group_gather(prep(jnp.transpose(routes[0], (0, 2, 1)), cot, capacity), bits)
        packs, h_attn = qkv(x, gain_one, weights, own_table, shard, n)
        packs = lax.all_to_all(packs, "ctx", split_axis=0, concat_axis=0, tiled=True).reshape(n, 2, rows, PACK)
        attn, lse, full = attn_forward(ends, packs, length)
        attn = lax.all_to_all(attn.reshape(n, tokens, 128), "ctx", split_axis=0, concat_axis=0, tiled=True)
        middle, h_ffn = middle_step(attn, wo, x, gain_two)
        xs, gs, gates = gather_rows(first, group_gather(h_ffn, bits), cxs, jnp.transpose(wr), number, capp)
        slots = cxs[:, tokens:]
    xs, gs, gates = merge(xs), merge(gs), merge(gates)
    pieces, outs, back, dgates = expert_step(base, xs, gs, gates, w_gate, w_up, w_down)
    y_part, gx_part = combine(first, slots, outs, back, dgates, tokens, capp)
    pieces = pieces.reshape(number * 6, PIECE, PIECE)
    gx = group_reduce(gx_part, bits)
    grad_middle, dwo, grad_attn, dwr, dgain_two = home_step(gx, h_ffn, middle, cot, wr, wo, gain_two, attn)
    grad_attn = lax.all_to_all(grad_attn, "ctx", split_axis=0, concat_axis=0, tiled=True).reshape(n, 2, rows, 128)
    grads = attn_backward(ends, packs, grad_attn, lse, full, table, length)
    grads = lax.all_to_all(grads.reshape(n, tokens, PACK), "ctx", split_axis=0, concat_axis=0, tiled=True)
    dw, grad_x, dgain_one = final_step(grads, weights, h_attn, x, gain_one, grad_middle, shard)
    mixed = middle + RESIDUAL * group_reduce(y_part, bits).astype(F32)
    own = line_sum(pieces, n)
    other = swap(own, "ctx", 1)
    scatter = lambda a: lax.psum(lax.psum_scatter(a, "fsdp", scatter_dimension=0, tiled=True), "ctx").astype(F32)
    dwo = scatter(dwo)[:, :head_lanes, :].reshape(shard, width)
    small = jnp.concatenate([dwr[:, :EXPERTS], dgain_two.reshape(width, 1).astype(BF16)], 1)
    small = scatter(jnp.pad(small, ((0, 0), (0, 127 - EXPERTS))))
    dwr, dgain_two = small[:, :EXPERTS], small[:, EXPERTS]
    dw = scatter(dw).reshape(shard, n, PACK)
    dgain_one = scatter(dgain_one.reshape(width).astype(BF16))

    outs = widen(index, own, other, [w.shape for w in (w_gate, w_up, w_down)])
    fold = lambda a: a.reshape(shard, KEY_VALUE_HEADS, copies, HEAD_DIMENSION).sum(2).reshape(shard, -1)
    return (
        mixed.reshape(inputs.shape),
        grad_x.reshape(inputs.shape),
        dgain_one,
        dgain_two,
        dw[:, :, :head_lanes].reshape(shard, -1),
        fold(dw[:, :, 128:192]),
        fold(dw[:, :, 192:256]),
        dwo,
        dwr,
        outs[0],
        outs[1],
        outs[2],
    )


def solution(mesh):
    tokens = P("fsdp", None, "ctx", None)
    one, two, three = P("fsdp"), P("fsdp", None), P("fsdp", None, None)
    return jax.shard_map(
        local,
        mesh=mesh,
        in_specs=(tokens, tokens, two, tokens, one, one, two, two, two, two, two, three, three, three),
        out_specs=(tokens, tokens, one, one, two, two, two, two, two, three, three, three),
        check_vma=False,
    )
```

profile of v0, /device:TPU:0, one launch (start us, length us, event | category | flops | bytes accessed | tf_op | source)
XLA Modules:
  0.0 551.0 jit_solution(10001739399873782904)
XLA Ops:
  0.6 0.7 stack.21
  1.3 0.7 stack.22
  2.0 0.6 pad_maximum_fusion.gain_ref
  2.5 56.5 %front.1 = (bf16[8,256,256]{2,1,0:T(8,128)(2,1)}, bf16[256,1024]{1,0:T(8,128)(2,1)}, bf16[2,4,288,1024]{3,2,1,0:T(8,128)(2,1)}, bf16[4,2,128,1024]{3,2,1,0:T(8,1...) custom-call(bf16[256,1024]{1,0:T(8,128)(2,1)} %wq_ref.1, ...), custom_call_target="tpu_custom_call" | custom-call | flops 2000000000 | bytes 50000000 | tf_op jit(solution)/shard_map/front/pallas_call | solution.py:1043
  59.0 25.4 %attend.1 = (bf16[8,2,128,128]{3,2,1,0:T(8,128)(2,1)}, f32[8,1,512]{2,1,0:T(1,128)}, f32[8,128,512]{2,1,0:T(8,128)}, bf16[4,288,1024]{2,1,0:T(8,128)(2,1)}) custom-call(s32[1,4]{1,0:T(1,128)} %ends_ref.3, bf16[8,2,128,256]{3,2,1,0:T(8,128)(2,1)} %bitcast.45, bf16[8,2,128,256]{3,2,1,0:T(8,128)(2,1)} %bitcast.46, bf16[2,288,1024]{2,1,0:T(8,128)(2,1)} %get-tuple-element.47.cxs_ref), custom_call_target="tpu_custom_call" | custom-call | flops 15000000512 | bytes 20000000 | tf_op jit(solution)/shard_map/attend/pallas_call | solution.py:1116
  84.4 41.7 %mid_step.1 = (f32[256,1024]{1,0:T(8,128)}, bf16[256,1024]{1,0:T(8,128)(2,1)}, bf16[8,256,128]{2,1,0:T(8,128)(2,1)}, bf16[4,8,80,1024]{3,2,1,0:T(8,128)(2,1)}, b...) custom-call(bf16[8,256,128]{2,1,0:T(8,128)(2,1)} %bitcast.48, ...), custom_call_target="tpu_custom_call" | custom-call | flops 4000000000 | bytes 50000000 | tf_op jit(solution)/shard_map/mid_step/pallas_call | solution.py:1293
  126.2 395.1 %backward_step.1 = (bf16[52,256,512]{2,1,0:T(8,128)(2,1)}, bf16[52,256,512]{2,1,0:T(8,128)(2,1)}, bf16[24,512,512]{2,1,0:T(8,128)(2,1)}, bf16[4,640,1024]{2,1,0:...) custom-call(s32[1,4]{1,0:T(1,128)} %ends_ref.3, ...), custom_call_target="tpu_custom_call" | custom-call | flops 60000002048 | bytes 1000000000 | tf_op jit(solution)/shard_map/backward_step/pallas_call | solution.py:2124
  521.3 0.6 pad_add_fusion.index_ref
  521.9 28.6 %tail.1 = (f32[8,1024,512]{2,1,0:T(8,128)}, f32[8,1024,512]{2,1,0:T(8,128)}, f32[8,512,1024]{2,1,0:T(8,128)}, f32[256,1024]{1,0:T(8,128)}, f32[256,1024]{1,0:T(8...) custom-call(s32[2]{0:T(128)} %pad_add_fusion.index_ref, ...), custom_call_target="tpu_custom_call" | custom-call | bytes 100000000 | tf_op jit(solution)/shard_map/tail/pallas_call | solution.py:762
where the time goes:
time: 560 us; the launch traced here: 551 us
  Pallas kernels  547 us (98%)
    pallas_call x1, Pallas kernels, backward_step(): pl.pallas_call(functools.partial(backward_kernel, n, length, capp), in_sp...  395 us
    pallas_call x1, Pallas kernels, front(): pl.pallas_call(functools.partial(front_kernel, n, cap), in_specs=[vmem, v...  56.5 us
    pallas_call x1, Pallas kernels, mid_step(): pl.pallas_call(functools.partial(mid_kernel, n, number, capp), in_specs=[...  41.7 us
    pallas_call x1, Pallas kernels, tail(): pl.pallas_call(functools.partial(tail_kernel, number), grid_spec=pltpu.Pr...  28.6 us
    pallas_call x1, Pallas kernels, attend(): pl.pallas_call(functools.partial(attend_kernel, length, n), grid=(blocks,...  25.4 us

commit v1 on v0

--- a/solution.py
+++ b/solution.py
@@ -1164,20 +1164,15 @@
         refs = (cxs_ref.at[0], cxs_ref.at[1], rest_ref.at[0], diag_ref.at[0], rest_ref.at[1], rest_ref.at[2], rest_ref.at[3], diag_ref.at[1])
         return pltpu.make_async_copy(refs[order[step]], cx.at[step % 2], load_sems.at[step % 2])
 
-    cx_half = cxs_ref.shape[1] // 2
-
-    def cx_cross(i):
-        at = pl.ds(i * cx_half, cx_half)
-        src = cxs_ref.at[1, at] if i == 0 else rest_ref.at[0, at]
-        return send(src, diag_ref.at[0, at], cx_send.at[i], cx_recv.at[i], group[1 - i])
+    def cx_cross():
+        return send(rest_ref.at[0], diag_ref.at[0], cx_send.at[0], cx_recv.at[0], group[0])
 
     def cx_core():
-        return send(diag_ref.at[0], diag_ref.at[1], cx_send.at[2], cx_recv.at[2], core)
+        return send(diag_ref.at[0], diag_ref.at[1], cx_send.at[1], cx_recv.at[1], core)
 
     load(0).start()
     greet([core, group[0]] + [{"ctx": c} for c in others(n)])
-    for i in range(2):
-        cx_cross(i).start()
+    cx_cross().start()
     halves = [pl.ds(k * split, split) for k in range(2)]
     exchanges = [(attn_ref.at[:, halves[k]], arrived.at[:, halves[k]], exch_send.at[k], exch_recv.at[k], local_sems.at[4 + k], n) for k in range(2)]
     for exchange in exchanges:
@@ -1209,10 +1204,8 @@
         hs[0, at, :] = h
         for i in range(3):
             hop(i, k).start()
-        if k == 0:
-            for i in range(2):
-                cx_cross(i).wait_recv()
-            cx_core().start()
+    cx_cross().wait_recv()
+    cx_core().start()
     keep = pltpu.make_async_copy(arrived, kept_ref, local_sems.at[1])
     keep.start()
 
@@ -1276,7 +1269,7 @@
             copy.wait()
     for i in range(2):
         cross(i).wait_send()
-        cx_cross(i).wait_send()
+    cx_cross().wait_send()
     cx_core().wait_send()
     for i in range(3):
         for k in range(2):
@@ -1318,8 +1311,8 @@
             dma(3, 2),
             dma(2),
             dma(2),
-            dma(3),
-            dma(3),
+            dma(2),
+            dma(2),
             dma(3),
             dma(3),
             dma(6),
@@ -1333,7 +1326,7 @@
 
 
 RING = 12
-LAG_MIDDLE, LAG_ACROSS, LAG_END = 1, 2, 4
+LAG_MIDDLE, LAG_ACROSS, LAG_END = 1, 2, 3
 ORDER_X, ORDER_Y, ORDER_CORE = 1, 2, 4
 
 
@@ -1561,11 +1554,11 @@
     attn_hbm,
     x_hbm,
     h_attn_hbm,
-    h_ref,
-    middle_ref,
-    wr_ref,
-    gains_ref,
-    lse_ref,
+    h_hbm,
+    middle_hbm,
+    wr_hbm,
+    gains_hbm,
+    lse_hbm,
     own_ref,
     other_ref,
     pieces_ref,
@@ -1611,7 +1604,7 @@
     comb_sems,
     part_sems,
 ):
-    tokens, width = h_ref.shape
+    tokens, width = h_hbm.shape
     half = length // 2
     rows = tokens // 2
     shard = width // 4
@@ -1848,18 +1841,32 @@
             tick(at_tick[0])
             at_tick[0] += 1
 
-    def backward(packs, table, keys, values, keys_t, grad_q, grad_k, grad_v, acc, full_buf, ga, pack_out, wbuf, total, grad_middle, dgain, col, small, columns, cot, wo, attn, x_in, h_attn):
-        ws = GroupSum(small, PIECE, lands, None, sems(2), None, free, False, core, group)
+    def backward(packs, table, keys, values, keys_t, grad_q, grad_k, grad_v, acc, full_buf, ga, pack_out, wbuf, total, grad_middle, dgain, col, small, columns, cot, wo, attn, x_in, h_attn, h_ref, middle_ref, wr_ref, gains_ref, lse_ref):
+        ws = GroupSum(small, small.shape[1], lands, None, sems(2), None, free, False, core, group)
         cs = GroupSum(columns, PIECE + 16, lands, None, sems(3), None, free, False, core, group)
         copies = [
             pltpu.make_async_copy(src, dst, local_sems.at[4 + k])
             for k, (src, dst) in enumerate(
-                ((cot_hbm, cot), (wo_hbm, wo), (attn_hbm, attn), (packs_hbm, packs), (table_hbm, table), (x_hbm, x_in), (h_attn_hbm, h_attn))
+                (
+                    (cot_hbm, cot),
+                    (wo_hbm, wo),
+                    (attn_hbm, attn),
+                    (packs_hbm, packs),
+                    (table_hbm, table),
+                    (x_hbm, x_in),
+                    (h_attn_hbm, h_attn),
+                    (h_hbm, h_ref),
+                    (middle_hbm, middle_ref),
+                    (wr_hbm, wr_ref),
+                    (gains_hbm, gains_ref),
+                    (lse_hbm, lse_ref),
+                )
             )
         ]
         for copy in copies:
             copy.start()
-        small[:, PIECE // 2 : PIECE, :] = jnp.zeros((8, PIECE // 2, PIECE), BF16)
+        small[:, 256:384, :] = jnp.zeros((8, 128, PIECE), BF16)
+        late_pieces[384:PIECE, :] = jnp.zeros((PIECE - 384, PIECE), BF16)
         columns[:, PIECE:, :] = jnp.zeros((8, 16, PIECE), BF16)
         go_on(2)
         gx.over_x(go_on)
@@ -1868,6 +1875,8 @@
         arrived = jnp.concatenate([arrived[:ext], arrived[ext:]], 1)
         gx.release()
 
+        for copy in copies[7:]:
+            copy.wait()
         h = h_ref[...]
         gain = gains_ref[1:2]
         extra = arrived[tokens:, :]
@@ -2009,7 +2018,7 @@
         ys.over_x()
         go_on(2)
         total[...] = jnp.zeros_like(total)
-        late_pieces[:PIECE] = ws.finish().astype(BF16)
+        late_pieces[:384] = ws.finish().astype(BF16)
         ws.release()
         ffn = ys.finish()
         mixed_ref[...] = middle_ref[...] + RESIDUAL * jnp.concatenate([ffn[:tokens], ffn[tokens:]], 1)
@@ -2084,13 +2093,18 @@
         f32(tokens, width),
         f32(8, width),
         bf(width, PACK),
-        bf(8, PIECE, PIECE),
+        bf(8, 384, PIECE),
         bf(8, PIECE + 16, PIECE),
         f32(tokens, width),
         bf(*wo_hbm.shape),
         bf(*attn_hbm.shape),
         f32(tokens, width),
         bf(tokens, width),
+        bf(tokens, width),
+        f32(tokens, width),
+        bf(*wr_hbm.shape),
+        f32(*gains_hbm.shape),
+        f32(*lse_hbm.shape),
     )
 
     def rest(t, carry):
@@ -2123,7 +2137,7 @@
     land_rows = max(2 * (tokens + EXPERTS), PIECE + 16)
     return pl.pallas_call(
         functools.partial(backward_kernel, n, length, capp),
-        in_specs=[smem] + [hbm] * 18 + [vmem] * 5,
+        in_specs=[smem] + [hbm] * 23,
         out_specs=[hbm] * 7 + [vmem, vmem],
         out_shape=[
             shaped((count,) + piece),
@@ -2165,7 +2179,7 @@
             dma(4, 6, 4),
             dma(2),
             pltpu.SemaphoreType.REGULAR((3,)),
-            dma(11),
+            dma(16),
             dma(2),
             dma(2, 2),
             dma(2, 6),

time: 560 us -> 568 us (1.014)
  Pallas kernels: 547 us -> 556 us
    pallas_call x1, Pallas kernels: 395 us -> 406 us  [backward_step(): pl.pallas_call(functools.partial(backward_kernel, n, length, capp), in_sp...]
where the time goes in v1:
time: 568 us; the launch traced here: 560 us
  Pallas kernels  556 us (98%)
    pallas_call x1, Pallas kernels, backward_step(): pl.pallas_call(functools.partial(backward_kernel, n, length, capp), in_sp...  406 us
    pallas_call x1, Pallas kernels, front(): pl.pallas_call(functools.partial(front_kernel, n, cap), in_specs=[vmem, v...  56.5 us
    pallas_call x1, Pallas kernels, mid_step(): pl.pallas_call(functools.partial(mid_kernel, n, number, capp), in_specs=[...  39.6 us
    pallas_call x1, Pallas kernels, tail(): pl.pallas_call(functools.partial(tail_kernel, number), grid_spec=pltpu.Pr...  28.6 us
    pallas_call x1, Pallas kernels, attend(): pl.pallas_call(functools.partial(attend_kernel, length, n), grid=(blocks,...  25.4 us

profile of v1, /device:TPU:0, one launch (start us, length us, event | category | flops | bytes accessed | tf_op | source)
XLA Modules:
  0.0 559.7 jit_solution(17357604392345328934)
XLA Ops:
  0.6 0.7 stack.21
  1.3 0.7 stack.22
  2.0 0.6 pad_maximum_fusion.gain_ref
  2.5 56.5 %front.1 = (bf16[8,256,256]{2,1,0:T(8,128)(2,1)}, bf16[256,1024]{1,0:T(8,128)(2,1)}, bf16[2,4,288,1024]{3,2,1,0:T(8,128)(2,1)}, bf16[4,2,128,1024]{3,2,1,0:T(8,1...) custom-call(bf16[256,1024]{1,0:T(8,128)(2,1)} %wq_ref.1, ...), custom_call_target="tpu_custom_call" | custom-call | flops 2000000000 | bytes 50000000 | tf_op jit(solution)/shard_map/front/pallas_call | solution.py:1043
  59.0 25.4 %attend.1 = (bf16[8,2,128,128]{3,2,1,0:T(8,128)(2,1)}, f32[8,1,512]{2,1,0:T(1,128)}, f32[8,128,512]{2,1,0:T(8,128)}, bf16[4,288,1024]{2,1,0:T(8,128)(2,1)}) custom-call(s32[1,4]{1,0:T(1,128)} %ends_ref.3, bf16[8,2,128,256]{3,2,1,0:T(8,128)(2,1)} %bitcast.45, bf16[8,2,128,256]{3,2,1,0:T(8,128)(2,1)} %bitcast.46, bf16[2,288,1024]{2,1,0:T(8,128)(2,1)} %get-tuple-element.47.cxs_ref), custom_call_target="tpu_custom_call" | custom-call | flops 15000000512 | bytes 20000000 | tf_op jit(solution)/shard_map/attend/pallas_call | solution.py:1116
  84.4 39.6 %mid_step.1 = (f32[256,1024]{1,0:T(8,128)}, bf16[256,1024]{1,0:T(8,128)(2,1)}, bf16[8,256,128]{2,1,0:T(8,128)(2,1)}, bf16[4,8,80,1024]{3,2,1,0:T(8,128)(2,1)}, b...) custom-call(bf16[8,256,128]{2,1,0:T(8,128)(2,1)} %bitcast.48, ...), custom_call_target="tpu_custom_call" | custom-call | flops 4000000000 | bytes 50000000 | tf_op jit(solution)/shard_map/mid_step/pallas_call | solution.py:1286
  124.0 405.9 %backward_step.1 = (bf16[52,256,512]{2,1,0:T(8,128)(2,1)}, bf16[52,256,512]{2,1,0:T(8,128)(2,1)}, bf16[24,512,512]{2,1,0:T(8,128)(2,1)}, bf16[4,640,1024]{2,1,0:...) custom-call(s32[1,4]{1,0:T(1,128)} %ends_ref.3, ...), custom_call_target="tpu_custom_call" | custom-call | flops 60000002048 | bytes 1000000000 | tf_op jit(solution)/shard_map/backward_step/pallas_call | solution.py:2138
  530.0 0.6 pad_add_fusion.index_ref
  530.6 28.6 %tail.1 = (f32[8,1024,512]{2,1,0:T(8,128)}, f32[8,1024,512]{2,1,0:T(8,128)}, f32[8,512,1024]{2,1,0:T(8,128)}, f32[256,1024]{1,0:T(8,128)}, f32[256,1024]{1,0:T(8...) custom-call(s32[2]{0:T(128)} %pad_add_fusion.index_ref, ...), custom_call_target="tpu_custom_call" | custom-call | bytes 100000000 | tf_op jit(solution)/shard_map/tail/pallas_call | solution.py:762

commit v2 on v1

--- a/solution.py
+++ b/solution.py
@@ -249,8 +249,9 @@
     result = acc[...] / total
     full_ref[0] = result
     lse_ref[0] = peak + jnp.log(total)
-    folded = fold_heads(jnp.transpose(result)).astype(BF16)
-    out_ref[...] = folded.reshape(out_ref.shape)
+    if out_ref is not None:
+        folded = fold_heads(jnp.transpose(result)).astype(BF16)
+        out_ref[...] = folded.reshape(out_ref.shape)
 
 
 def attn_forward(ends, packs, length):
@@ -1073,10 +1074,71 @@
     )(wq, wk, wv, wo_part, wr, gains, x, table, routes, cot)
 
 
-def attend_kernel(length, n, ends_ref, q_ref, pack_ref, cxs_ref, out_ref, lse_ref, full_ref, rest_ref, keys, values_t, acc, near_send, near_recv, core_send, core_recv):
+def attend_kernel(
+    length,
+    n,
+    number,
+    capp,
+    ends_ref,
+    q_ref,
+    pack_ref,
+    cxs_ref,
+    wo_hbm,
+    wr_ref,
+    x_hbm,
+    gain_ref,
+    lse_ref,
+    full_ref,
+    middle_ref,
+    h_ref,
+    kept_ref,
+    xs_ref,
+    gs_ref,
+    gates_ref,
+    rest_ref,
+    diag_ref,
+    keys,
+    values_t,
+    acc,
+    result,
+    arrived,
+    hs,
+    wo_ref,
+    x_ref,
+    cx,
+    rows_out,
+    grads_out,
+    gates_out,
+    near_send,
+    near_recv,
+    core_send,
+    core_recv,
+    exch_send,
+    exch_recv,
+    hop_send,
+    hop_recv,
+    cross_send,
+    cross_recv,
+    cx_send,
+    cx_recv,
+    fwd_send,
+    fwd_recv,
+    local_sems,
+    own_sems,
+    load_sems,
+    store_sems,
+):
     block = pl.program_id(0)
+    last = pl.num_programs(0) - 1
+    tokens, width = x_ref.shape
+    split = tokens // 2
+    per = BLK // split
+    per_half = length // BLK // 2
+    ctx, fsdp = lax.axis_index("ctx"), lax.axis_index("fsdp")
+    first = (fsdp * 2 + lax.rem(ctx, 2)) * number
     core, group = neighbours()
     near = group[1]
+    copies = [pltpu.make_async_copy(wo_hbm, wo_ref, local_sems.at[0]), pltpu.make_async_copy(x_hbm, x_ref, local_sems.at[1])]
 
     def to_near():
         return send(cxs_ref.at[0], rest_ref.at[0], near_send.at[0], near_recv.at[0], near)
@@ -1085,219 +1147,229 @@
         src = cxs_ref.at[i] if i < 2 else rest_ref.at[0]
         return send(src, rest_ref.at[1 + i], core_send.at[i], core_recv.at[i], core)
 
+    def cx_cross():
+        return send(rest_ref.at[0], diag_ref.at[0], cx_send.at[0], cx_recv.at[0], group[0])
+
+    def cx_core():
+        return send(diag_ref.at[0], diag_ref.at[1], cx_send.at[1], cx_recv.at[1], core)
+
+    def to_home(c, late):
+        at = pl.ds(pl.multiple_of(late * split, split), split)
+        d = lax.rem(c - ctx + n - 1, n)
+        return send(result.at[c, at], arrived.at[ctx, at], exch_send.at[late, d], exch_recv.at[late, d], {"ctx": c})
+
+    def from_device(c, late):
+        at = pl.ds(late * split, split)
+        d = lax.rem(ctx - c + n - 1, n)
+        return send(result.at[c, at], arrived.at[c, at], exch_send.at[late, d], exch_recv.at[late, d], {"ctx": c})
+
+    def own_rows(late):
+        at = pl.ds(pl.multiple_of(late * split, split), split)
+        return pltpu.make_async_copy(result.at[ctx, at], arrived.at[ctx, at], own_sems.at[late])
+
     @pl.when(block == 0)
     def _():
-        greet([core, near])
+        for copy in copies:
+            copy.start()
+        greet([core, group[0]] + [{"ctx": c} for c in others(n)])
         to_near().start()
         for i in range(2):
             to_core(i).start()
 
-    attn_forward_kernel(length, ends_ref, q_ref, pack_ref, out_ref, lse_ref, full_ref, keys, values_t, acc)
-
-    @pl.when(block == pl.num_programs(0) - 2)
+    attn_forward_kernel(length, ends_ref, q_ref, pack_ref, None, lse_ref, full_ref, keys, values_t, acc)
+    late = block // per_half
+    folded = fold_heads(jnp.transpose(full_ref[0])).astype(BF16)
+    for k in range(per):
+        c = lax.rem(block, per_half) * per + k
+        result[c, pl.ds(pl.multiple_of(late * split, split), split), :] = folded[k * split : (k + 1) * split]
+
+        @pl.when(c == ctx)
+        def _():
+            own_rows(late).start()
+
+        @pl.when(c != ctx)
+        def _():
+            to_home(c, late).start()
+
+    @pl.when(block == last - 1)
     def _():
         to_near().wait_recv()
         to_core(2).start()
-
-    @pl.when(block == pl.num_programs(0) - 1)
+        cx_cross().start()
+
+    @pl.when(block == last)
     def _():
+        order = (0, 4, 1, 2, 3, 5, 6, 7)
+        halves = [pl.ds(k * split, split) for k in range(2)]
+
+        def load(step):
+            refs = (cxs_ref.at[0], cxs_ref.at[1], rest_ref.at[0], diag_ref.at[0], rest_ref.at[1], rest_ref.at[2], rest_ref.at[3], diag_ref.at[1])
+            return pltpu.make_async_copy(refs[order[step]], cx.at[step % 2], load_sems.at[step % 2])
+
+        def hop(i, k):
+            return send(hs.at[0, halves[k]], hs.at[(1, 2, 4)[i], halves[k]], hop_send.at[i, k], hop_recv.at[i, k], (group[0], group[1], core)[i])
+
+        def cross(i):
+            return send(hs.at[1 + i, halves[i]], hs.at[3, halves[i]], cross_send.at[i], cross_recv.at[i], group[1 - i])
+
+        def forward(i):
+            return send(hs.at[1 + i], hs.at[5 + i], fwd_send.at[i], fwd_recv.at[i], core)
+
+        load(0).start()
         for i in range(3):
-            to_core(i).wait()
+            to_core(i).wait_recv()
+        load(1).start()
+        for copy in copies:
+            copy.wait()
+        for k in range(2):
+            own_rows(k).wait()
+            for d in range(1, n):
+                from_device(lax.rem(ctx + d, n), k).wait_recv()
+            at = slice(k * split, (k + 1) * split)
+            total = None
+            for c in range(n):
+                part = dot(arrived[c, at, :], wo_ref[c])
+                total = part if total is None else total + part
+            middle = x_ref[at, :] + RESIDUAL * total
+            middle_ref[at, :] = middle
+            normed, _ = norm_parts(middle)
+            h = (normed * gain_ref[1:2]).astype(BF16)
+            h_ref[at, :] = h
+            hs[0, at, :] = h
+            for i in range(3):
+                hop(i, k).start()
+        keep = pltpu.make_async_copy(arrived, kept_ref, local_sems.at[2])
+        keep.start()
+
+        def stores(step):
+            b = order[step]
+            pairs = ((rows_out, xs_ref), (grads_out, gs_ref), (gates_out, gates_ref))
+            return [pltpu.make_async_copy(src.at[step % 2], dst.at[:, b], store_sems.at[step % 2, k]) for k, (src, dst) in enumerate(pairs)]
+
+        def place(step):
+            b, slot = order[step], step % 2
+            load(step).wait()
+            if step >= 2:
+                for copy in stores(step - 2):
+                    copy.wait()
+            h = hs[b]
+            logits = jnp.transpose(dot(h, wr_ref[...]))[:EXPERTS, :]
+            raw = jnp.exp(logits - jnp.max(logits, 0, keepdims=True))
+            router = raw / jnp.sum(raw, 0, keepdims=True)
+            slots = cx[slot, tokens:, :tokens].astype(F32)
+            hots = one_hot(slots, first, number, capp)
+            places = jnp.concatenate(hots, 0).astype(BF16)
+            rows = dot(places, h).astype(BF16)
+            grads = dot(places, cx[slot, :tokens, :]).astype(BF16)
+            for j in range(number):
+                at = slice(j * capp, (j + 1) * capp)
+                rows_out[slot, j] = rows[at]
+                grads_out[slot, j] = grads[at]
+                gate = jnp.sum(hots[j] * own_row(router, first + j), 1, keepdims=True)
+                gates_out[slot, j] = jnp.broadcast_to(gate, (capp, 128))
+            for copy in stores(step):
+                copy.start()
+            if step + 2 < 8:
+                if step + 2 == 4:
+                    cx_cross().wait_recv()
+                    cx_core().start()
+                if step + 2 == 7:
+                    cx_core().wait_recv()
+                load(step + 2).start()
+
+        place(0)
+        for k in range(2):
+            hop(2, k).wait_recv()
+        place(1)
+        hop(0, 0).wait_recv()
+        cross(0).start()
+        hop(1, 0).wait_recv()
+        hop(1, 1).wait_recv()
+        cross(1).start()
+        forward(1).start()
+        hop(0, 1).wait_recv()
+        forward(0).start()
+        place(2)
+        place(3)
+        for i in range(2):
+            cross(i).wait_recv()
+        forward(2).start()
+        place(4)
+        for i in range(3):
+            forward(i).wait_recv()
+            place(5 + i)
+        for step in (6, 7):
+            for copy in stores(step):
+                copy.wait()
+        for k in range(2):
+            for d in range(1, n):
+                to_home(lax.rem(ctx + d, n), k).wait_send()
+        for i in range(2):
+            cross(i).wait_send()
+        cx_cross().wait_send()
+        cx_core().wait_send()
+        for i in range(3):
+            for k in range(2):
+                hop(i, k).wait_send()
+            forward(i).wait_send()
+            to_core(i).wait_send()
         to_near().wait_send()
-
-
-def attend(ends, packs, cxs, length):
+        keep.wait()
+
+
+def attend(ends, packs, cxs, wo, wr, x, gains, length, number, capp):
     n, _, rows, _ = packs.shape
+    tokens, width = x.shape
     blocks, per = length // BLK, BLK // rows
     per_half = blocks // 2
     tiles = lambda i: (lax.rem(i, per_half), i // per_half, 0, 0)
     hbm = pl.BlockSpec(memory_space=pl.ANY)
-    dma = lambda k: pltpu.SemaphoreType.DMA((k,))
+    dma = lambda *k: pltpu.SemaphoreType.DMA(k)
+    same = lambda shape: pl.BlockSpec(shape, lambda i: (0,) * len(shape))
+    shaped = lambda shape, dtype=BF16: jax.ShapeDtypeStruct(shape, dtype)
     return pl.pallas_call(
-        functools.partial(attend_kernel, length, n),
+        functools.partial(attend_kernel, length, n, number, capp),
         grid=(blocks,),
         in_specs=[
             pl.BlockSpec(memory_space=pltpu.SMEM),
             pl.BlockSpec((per, 1, rows, PACK), tiles),
-            pl.BlockSpec(packs.shape, lambda i: (0, 0, 0, 0)),
+            same(packs.shape),
+            hbm,
+            hbm,
+            same(wr.shape),
+            hbm,
+            same(gains.shape),
+        ],
+        out_specs=[
+            pl.BlockSpec((1, 1, 2 * BLK), lambda i: (i, 0, 0)),
+            pl.BlockSpec((1, 128, 2 * BLK), lambda i: (i, 0, 0)),
+            same((tokens, width)),
+            same((tokens, width)),
+            hbm,
+            hbm,
+            hbm,
+            hbm,
+            hbm,
             hbm,
         ],
-        out_specs=[
-            pl.BlockSpec((per, 1, rows, 128), tiles),
-            pl.BlockSpec((1, 1, 2 * BLK), lambda i: (i, 0, 0)),
-            pl.BlockSpec((1, 128, 2 * BLK), lambda i: (i, 0, 0)),
-            hbm,
+        out_shape=[
+            shaped((blocks, 1, 2 * BLK), F32),
+            shaped((blocks, 128, 2 * BLK), F32),
+            shaped((tokens, width), F32),
+            shaped((tokens, width)),
+            shaped((n, tokens, 128)),
+            shaped((number, 8, capp, width)),
+            shaped((number, 8, capp, width)),
+            shaped((number, 8, capp, 128), F32),
+            shaped((4,) + cxs.shape[1:]),
+            shaped((2,) + cxs.shape[1:]),
         ],
         scratch_shapes=[
             pltpu.VMEM((length, 128), BF16),
             pltpu.VMEM((128, length), BF16),
             pltpu.VMEM((128, 2 * BLK), F32),
-            dma(1),
-            dma(1),
-            dma(3),
-            dma(3),
-        ],
-        out_shape=[
-            jax.ShapeDtypeStruct((n, 2, rows, 128), BF16),
-            jax.ShapeDtypeStruct((blocks, 1, 2 * BLK), F32),
-            jax.ShapeDtypeStruct((blocks, 128, 2 * BLK), F32),
-            jax.ShapeDtypeStruct((4,) + cxs.shape[1:], BF16),
-        ],
-        compiler_params=params(collective_id=3, has_side_effects=True),
-        cost_estimate=cost(1.5e10, 2e7),
-        name="attend",
-    )(ends, packs, packs, cxs)
-
-
-def mid_kernel(n, number, capp, attn_ref, cxs_ref, rest_ref, wo_hbm, wr_ref, x_hbm, gain_ref, middle_ref, h_ref, kept_ref, xs_ref, gs_ref, gates_ref, diag_ref, arrived, hs, wo_ref, x_ref, cx, rows_out, grads_out, gates_out, exch_send, exch_recv, hop_send, hop_recv, cross_send, cross_recv, cx_send, cx_recv, fwd_send, fwd_recv, local_sems, load_sems, store_sems):
-    tokens, width = x_ref.shape
-    split = tokens // 2
-    ctx, fsdp = lax.axis_index("ctx"), lax.axis_index("fsdp")
-    first = (fsdp * 2 + lax.rem(ctx, 2)) * number
-    core, group = neighbours()
-    copies = [pltpu.make_async_copy(wo_hbm, wo_ref, local_sems.at[2]), pltpu.make_async_copy(x_hbm, x_ref, local_sems.at[3])]
-    for copy in copies:
-        copy.start()
-    order = (0, 4, 1, 2, 3, 5, 6, 7)
-
-    def load(step):
-        refs = (cxs_ref.at[0], cxs_ref.at[1], rest_ref.at[0], diag_ref.at[0], rest_ref.at[1], rest_ref.at[2], rest_ref.at[3], diag_ref.at[1])
-        return pltpu.make_async_copy(refs[order[step]], cx.at[step % 2], load_sems.at[step % 2])
-
-    def cx_cross():
-        return send(rest_ref.at[0], diag_ref.at[0], cx_send.at[0], cx_recv.at[0], group[0])
-
-    def cx_core():
-        return send(diag_ref.at[0], diag_ref.at[1], cx_send.at[1], cx_recv.at[1], core)
-
-    load(0).start()
-    greet([core, group[0]] + [{"ctx": c} for c in others(n)])
-    cx_cross().start()
-    halves = [pl.ds(k * split, split) for k in range(2)]
-    exchanges = [(attn_ref.at[:, halves[k]], arrived.at[:, halves[k]], exch_send.at[k], exch_recv.at[k], local_sems.at[4 + k], n) for k in range(2)]
-    for exchange in exchanges:
-        exchange_start(*exchange)
-    for copy in copies:
-        copy.wait()
-
-    def hop(i, k):
-        return send(hs.at[0, halves[k]], hs.at[(1, 2, 4)[i], halves[k]], hop_send.at[i, k], hop_recv.at[i, k], (group[0], group[1], core)[i])
-
-    def cross(i):
-        return send(hs.at[1 + i, halves[i]], hs.at[3, halves[i]], cross_send.at[i], cross_recv.at[i], group[1 - i])
-
-    def forward(i):
-        return send(hs.at[1 + i], hs.at[5 + i], fwd_send.at[i], fwd_recv.at[i], core)
-
-    for k in range(2):
-        exchange_wait(*exchanges[k])
-        at = slice(k * split, (k + 1) * split)
-        total = None
-        for c in range(n):
-            part = dot(arrived[c, at, :], wo_ref[c])
-            total = part if total is None else total + part
-        middle = x_ref[at, :] + RESIDUAL * total
-        middle_ref[at, :] = middle
-        normed, _ = norm_parts(middle)
-        h = (normed * gain_ref[1:2]).astype(BF16)
-        h_ref[at, :] = h
-        hs[0, at, :] = h
-        for i in range(3):
-            hop(i, k).start()
-    cx_cross().wait_recv()
-    cx_core().start()
-    keep = pltpu.make_async_copy(arrived, kept_ref, local_sems.at[1])
-    keep.start()
-
-    def stores(step):
-        b = order[step]
-        pairs = ((rows_out, xs_ref), (grads_out, gs_ref), (gates_out, gates_ref))
-        return [pltpu.make_async_copy(src.at[step % 2], dst.at[:, b], store_sems.at[step % 2, k]) for k, (src, dst) in enumerate(pairs)]
-
-    def place(step):
-        b, slot = order[step], step % 2
-        load(step).wait()
-        if step >= 2:
-            for copy in stores(step - 2):
-                copy.wait()
-        h = hs[b]
-        logits = jnp.transpose(dot(h, wr_ref[...]))[:EXPERTS, :]
-        raw = jnp.exp(logits - jnp.max(logits, 0, keepdims=True))
-        router = raw / jnp.sum(raw, 0, keepdims=True)
-        slots = cx[slot, tokens:, :tokens].astype(F32)
-        hots = one_hot(slots, first, number, capp)
-        places = jnp.concatenate(hots, 0).astype(BF16)
-        rows = dot(places, h).astype(BF16)
-        grads = dot(places, cx[slot, :tokens, :]).astype(BF16)
-        for j in range(number):
-            at = slice(j * capp, (j + 1) * capp)
-            rows_out[slot, j] = rows[at]
-            grads_out[slot, j] = grads[at]
-            gate = jnp.sum(hots[j] * own_row(router, first + j), 1, keepdims=True)
-            gates_out[slot, j] = jnp.broadcast_to(gate, (capp, 128))
-        for copy in stores(step):
-            copy.start()
-        if step + 2 < 8:
-            if step + 2 == 7:
-                cx_core().wait_recv()
-            load(step + 2).start()
-
-    load(1).start()
-    place(0)
-    for k in range(2):
-        hop(2, k).wait_recv()
-    place(1)
-    hop(0, 0).wait_recv()
-    cross(0).start()
-    hop(1, 0).wait_recv()
-    hop(1, 1).wait_recv()
-    cross(1).start()
-    forward(1).start()
-    hop(0, 1).wait_recv()
-    forward(0).start()
-    place(2)
-    place(3)
-    for i in range(2):
-        cross(i).wait_recv()
-    forward(2).start()
-    place(4)
-    for i in range(3):
-        forward(i).wait_recv()
-        place(5 + i)
-    for step in (6, 7):
-        for copy in stores(step):
-            copy.wait()
-    for i in range(2):
-        cross(i).wait_send()
-    cx_cross().wait_send()
-    cx_core().wait_send()
-    for i in range(3):
-        for k in range(2):
-            hop(i, k).wait_send()
-        forward(i).wait_send()
-    keep.wait()
-
-
-def mid_step(attn, cxs, rest, wo, wr, x, gains, number, capp, n):
-    tokens, width = x.shape
-    hbm, vmem = pl.BlockSpec(memory_space=pl.ANY), pl.BlockSpec(memory_space=pltpu.VMEM)
-    dma = lambda *k: pltpu.SemaphoreType.DMA(k)
-    shaped = lambda shape, dtype=BF16: jax.ShapeDtypeStruct(shape, dtype)
-    return pl.pallas_call(
-        functools.partial(mid_kernel, n, number, capp),
-        in_specs=[hbm, hbm, hbm, hbm, vmem, hbm, vmem],
-        out_specs=[vmem, vmem, hbm, hbm, hbm, hbm, hbm],
-        out_shape=[
-            shaped((tokens, width), F32),
-            shaped((tokens, width)),
-            shaped(attn.shape),
-            shaped((number, 8, capp, width)),
-            shaped((number, 8, capp, width)),
-            shaped((number, 8, capp, 128), F32),
-            shaped((2,) + cxs.shape[1:]),
-        ],
-        scratch_shapes=[
-            pltpu.VMEM(attn.shape, BF16),
+            pltpu.VMEM((n, tokens, 128), BF16),
+            pltpu.VMEM((n, tokens, 128), BF16),
             pltpu.VMEM((8, tokens, width), BF16),
             pltpu.VMEM(wo.shape, BF16),
             pltpu.VMEM((tokens, width), F32),
@@ -1305,6 +1377,10 @@
             pltpu.VMEM((2, number, capp, width), BF16),
             pltpu.VMEM((2, number, capp, width), BF16),
             pltpu.VMEM((2, number, capp, 128), F32),
+            dma(1),
+            dma(1),
+            dma(3),
+            dma(3),
             dma(2, n - 1),
             dma(2, n - 1),
             dma(3, 2),
@@ -1315,18 +1391,19 @@
             dma(2),
             dma(3),
             dma(3),
-            dma(6),
+            dma(3),
+            dma(2),
             dma(2),
             dma(2, 3),
         ],
-        compiler_params=params(collective_id=2, has_side_effects=True),
-        cost_estimate=cost(4e9, 5e7),
-        name="mid_step",
-    )(attn, cxs, rest, wo, wr, x, gains)
+        compiler_params=params(collective_id=3, has_side_effects=True),
+        cost_estimate=cost(2e10, 7e7),
+        name="attend",
+    )(ends, packs, packs, cxs, wo, wr, x, gains)
 
 
 RING = 12
-LAG_MIDDLE, LAG_ACROSS, LAG_END = 1, 2, 3
+LAG_MIDDLE, LAG_ACROSS, LAG_END = 1, 2, 4
 ORDER_X, ORDER_Y, ORDER_CORE = 1, 2, 4
 
 
@@ -2257,8 +2334,7 @@
         )
         wo, wr = wo.reshape(n, 128, width), wr.reshape(width, 128)
         packs = packs.reshape(n, 2, rows, PACK)
-        attn, lse, full, cx_rest = attend(ends, packs, cxs, length)
-        middle, h_ffn, attn, xs, gs, gates, diag = mid_step(attn.reshape(n, tokens, 128), cxs, cx_rest, wo, wr, x, gains, number, capp, n)
+        lse, full, middle, h_ffn, attn, xs, gs, gates, cx_rest, diag = attend(ends, packs, cxs, wo, wr, x, gains, length, number, capp)
         own, other, _, _, _, _, _, grad_x, mixed = backward_step(
             ends,
             merge(xs),

time: 568 us -> 550 us (0.968)
  Pallas kernels: 556 us -> 538 us
    pallas_call x1, Pallas kernels: 406 us -> 392 us  [backward_step(): pl.pallas_call(functools.partial(backward_kernel, n, length, capp), in_sp...]
    pallas_call x2 -> x1, Pallas kernels: 65 us -> 60.6 us  [attend(): pl.pallas_call(functools.partial(attend_kernel, length, n, number, capp),...]
where the time goes in v2:
time: 550 us; the launch traced here: 541 us
  Pallas kernels  538 us (98%)
    pallas_call x1, Pallas kernels, backward_step(): pl.pallas_call(functools.partial(backward_kernel, n, length, capp), in_sp...  392 us
    pallas_call x1, Pallas kernels, attend(): pl.pallas_call(functools.partial(attend_kernel, length, n, number, capp),...  60.6 us
    pallas_call x1, Pallas kernels, front(): pl.pallas_call(functools.partial(front_kernel, n, cap), in_specs=[vmem, v...  56.5 us
    pallas_call x1, Pallas kernels, tail(): pl.pallas_call(functools.partial(tail_kernel, number), grid_spec=pltpu.Pr...  28.6 us

profile of v2, /device:TPU:0, one launch (start us, length us, event | category | flops | bytes accessed | tf_op | source)
XLA Modules:
  0.0 541.4 jit_solution(3459314133001510694)
XLA Ops:
  0.6 0.7 stack.21
  1.3 0.7 stack.22
  2.0 0.6 pad_maximum_fusion.gain_ref
  2.5 56.5 %front.1 = (bf16[8,256,256]{2,1,0:T(8,128)(2,1)}, bf16[256,1024]{1,0:T(8,128)(2,1)}, bf16[2,4,288,1024]{3,2,1,0:T(8,128)(2,1)}, bf16[4,2,128,1024]{3,2,1,0:T(8,1...) custom-call(bf16[256,1024]{1,0:T(8,128)(2,1)} %wq_ref.1, ...), custom_call_target="tpu_custom_call" | custom-call | flops 2000000000 | bytes 50000000 | tf_op jit(solution)/shard_map/front/pallas_call | solution.py:1044
  59.0 60.6 %attend.1 = (f32[8,1,512]{2,1,0:T(1,128)}, f32[8,128,512]{2,1,0:T(8,128)}, f32[256,1024]{1,0:T(8,128)}, bf16[256,1024]{1,0:T(8,128)(2,1)}, bf16[8,256,128]{2,1,0...) custom-call(s32[1,4]{1,0:T(1,128)} %ends_ref.3, ...), custom_call_target="tpu_custom_call" | custom-call | flops 20000000000 | bytes 70000000 | tf_op jit(solution)/shard_map/attend/pallas_call | solution.py:1330
  119.7 392.0 %backward_step.1 = (bf16[52,256,512]{2,1,0:T(8,128)(2,1)}, bf16[52,256,512]{2,1,0:T(8,128)(2,1)}, bf16[24,512,512]{2,1,0:T(8,128)(2,1)}, bf16[4,640,1024]{2,1,0:...) custom-call(s32[1,4]{1,0:T(1,128)} %ends_ref.3, ...), custom_call_target="tpu_custom_call" | custom-call | flops 60000002048 | bytes 1000000000 | tf_op jit(solution)/shard_map/backward_step/pallas_call | solution.py:2215
  511.7 0.6 pad_add_fusion.index_ref
  512.3 28.6 %tail.1 = (f32[8,1024,512]{2,1,0:T(8,128)}, f32[8,1024,512]{2,1,0:T(8,128)}, f32[8,512,1024]{2,1,0:T(8,128)}, f32[256,1024]{1,0:T(8,128)}, f32[256,1024]{1,0:T(8...) custom-call(s32[2]{0:T(128)} %pad_add_fusion.index_ref, ...), custom_call_target="tpu_custom_call" | custom-call | bytes 100000000 | tf_op jit(solution)/shard_map/tail/pallas_call | solution.py:763

commit v3 on v2

--- a/solution.py
+++ b/solution.py
@@ -689,10 +689,11 @@
         for chunk in range(2):
             columns = slice(chunk * part, (chunk + 1) * part)
             for half in range(2):
-                at = slice(half * PIECE, (half + 1) * PIECE)
-                gate_ref[0, at, columns] = ref[3 * chunk + half, :, :part].astype(F32)
-                up_ref[0, at, columns] = ref[3 * chunk + half, :, part:].astype(F32)
-                down_ref[0, columns, at] = ref[3 * chunk + 2, half * part : (half + 1) * part, :].astype(F32)
+                for q in range(2):
+                    at = slice(half * PIECE + q * 256, half * PIECE + (q + 1) * 256)
+                    gate_ref[0, at, columns] = ref[6 * chunk + 2 * half + q, :, :part].astype(F32)
+                    up_ref[0, at, columns] = ref[6 * chunk + 2 * half + q, :, part:].astype(F32)
+                down_ref[0, columns, half * PIECE : (half + 1) * PIECE] = ref[6 * chunk + 4 + half].astype(F32)
 
     @pl.when(pl.program_id(0) == 0)
     def _():
@@ -703,18 +704,18 @@
         write(other_ref)
 
 
-def tail_kernel(number, index_ref, own_ref, other_ref, own_small_ref, other_small_ref, mixed_in, grad_in, gate_ref, up_ref, down_ref, mixed_ref, grad_ref, dwq_ref, dwk_ref, dwv_ref, dwo_ref, dwr_ref, g1_ref, g2_ref):
+def tail_kernel(number, index_ref, own_ref, other_ref, own_small_ref, other_small_ref, own_rest_ref, other_rest_ref, mixed_in, grad_in, gate_ref, up_ref, down_ref, mixed_ref, grad_ref, dwq_ref, dwk_ref, dwv_ref, dwo_ref, dwr_ref, g1_ref, g2_ref):
     widen_kernel(number, index_ref, own_ref, other_ref, gate_ref, up_ref, down_ref)
     mixed_ref[...] = mixed_in[...]
     grad_ref[...] = grad_in[...]
 
     @pl.when((pl.program_id(0) == 0) & (pl.program_id(1) == 0))
     def _():
-        for which, ref in enumerate((own_small_ref, other_small_ref)):
+        for which, (ref, rest) in enumerate(((own_small_ref, own_rest_ref), (other_small_ref, other_rest_ref))):
             part = index_ref[which] // number
             at = pl.ds(pl.multiple_of(part * 128, 128), 128)
             for q in range(4):
-                block = ref[1, q * 128 : (q + 1) * 128, :].astype(F32)
+                block = ref[1 + q // 2, q % 2 * 128 : (q % 2 + 1) * 128, :].astype(F32)
                 dwq_ref[at, q * 256 : q * 256 + 128] = block[:, :128]
                 dwq_ref[at, q * 256 + 128 : (q + 1) * 256] = block[:, 256:384]
                 one, two = block[:, 128:256], block[:, 384:]
@@ -723,17 +724,18 @@
                 dwv_ref[at, q * 128 : (q + 1) * 128] = jnp.where(low, pltpu.roll(one, 64, 1), two)
             dwo_ref[at, :PIECE] = ref[0, 0:128, :].astype(F32)
             dwo_ref[at, PIECE:] = ref[0, 128:256, :].astype(F32)
-            dwr_ref[:, at] = jnp.transpose(ref[0, 256:384, :128].astype(F32))[:EXPERTS]
-            gains = ref[0, 384:400, :128].astype(F32)
-            g1_ref[pl.ds(part, 1), :] = gains[0:1]
-            g2_ref[pl.ds(part, 1), :] = gains[1:2]
+            low_rows = rest[0].astype(F32)
+            for q in range(EXPERTS // 8):
+                dwr_ref[q * 8 : (q + 1) * 8, at] = low_rows[:8, q * 128 : (q + 1) * 128]
+            g1_ref[pl.ds(part, 1), :] = low_rows[8:9, :128]
+            g2_ref[pl.ds(part, 1), :] = low_rows[9:10, :128]
 
 
 def expert_specs(number, shapes):
     last = number - 1
     ins = [
-        pl.BlockSpec((6, PIECE, PIECE), lambda s, e, at: (jnp.where(s == 0, e, last), 0, 0)),
-        pl.BlockSpec((6, PIECE, PIECE), lambda s, e, at: (jnp.where(s == 0, 0, e), 0, 0)),
+        pl.BlockSpec((12, PIECE // 2, PIECE), lambda s, e, at: (jnp.where(s == 0, e, last), 0, 0)),
+        pl.BlockSpec((12, PIECE // 2, PIECE), lambda s, e, at: (jnp.where(s == 0, 0, e), 0, 0)),
     ]
     outs = [pl.BlockSpec((1,) + tuple(shape[1:]), lambda s, e, at: (at[s] + e, 0, 0)) for shape in shapes]
     return ins, outs, [jax.ShapeDtypeStruct(shape, F32) for shape in shapes]
@@ -752,11 +754,12 @@
     )(index, own, other)
 
 
-def tail(index, own, other, mixed, grad_x, shapes, shard):
+def tail(index, own, other, own_rest, other_rest, mixed, grad_x, shapes, shard):
     number = shapes[0][0] // 2
     tokens, width = mixed.shape
     ins, outs, out_shapes = expert_specs(number, shapes)
-    small = pl.BlockSpec((2, PIECE, PIECE), lambda s, e, at: (3 * number, 0, 0))
+    small = pl.BlockSpec((3, PIECE // 2, PIECE), lambda s, e, at: (4 * number, 0, 0))
+    rest = pl.BlockSpec(own_rest.shape, lambda s, e, at: (0, 0, 0))
     rows = pl.BlockSpec((tokens // (2 * number), width), lambda s, e, at: (s * number + e, 0))
     small_shapes = [(shard, width), (shard, width // 2), (shard, width // 2), (shard, width), (EXPERTS, shard), (2, 128), (2, 128)]
     whole = [pl.BlockSpec(shape, lambda s, e, at: (0, 0)) for shape in small_shapes]
@@ -765,7 +768,7 @@
         grid_spec=pltpu.PrefetchScalarGridSpec(
             num_scalar_prefetch=1,
             grid=(2, number),
-            in_specs=ins + [small, small, rows, rows],
+            in_specs=ins + [small, small, rest, rest, rows, rows],
             out_specs=outs + [rows, rows] + whole,
         ),
         out_shape=out_shapes
@@ -774,7 +777,7 @@
         compiler_params=params(),
         cost_estimate=cost(0, 1e8),
         name="tail",
-    )(index, own, other, own, other, mixed, grad_x)
+    )(index, own, other, own, other, own_rest, other_rest, mixed, grad_x)
 
 
 def swap(value, axis, bit):
@@ -1591,14 +1594,14 @@
 
         @pl.when(self.middle)
         def _():
-            for i in range(count + LAG_MIDDLE - LAG_ACROSS - 4, count):
+            for i in range(max(0, count + LAG_MIDDLE - LAG_ACROSS - 4), count):
                 self.drain_middle(jnp.int32(i))
 
         @pl.when(jnp.logical_not(self.middle))
         def _():
-            for i in range(count - 3, count):
+            for i in range(max(0, count - 3), count):
                 self.send_line(self.mine.at[0], jnp.int32(i)).wait_send()
-            for i in range(count - LAG_END - 2, count):
+            for i in range(max(0, count - LAG_END - 2), count):
                 self.drain_end(jnp.int32(i))
 
         def arrived(i, carry):
@@ -1638,6 +1641,8 @@
     lse_hbm,
     own_ref,
     other_ref,
+    own_rest_ref,
+    other_rest_ref,
     pieces_ref,
     outs_ref,
     backs_ref,
@@ -1656,6 +1661,10 @@
     y_land_y,
     own_buf,
     late_pieces,
+    late_rest,
+    rest_inbox,
+    rest_across,
+    rest_mine,
     ga_in,
     grads_in,
     line_send,
@@ -1680,6 +1689,7 @@
     store_sems,
     comb_sems,
     part_sems,
+    rest_sems,
 ):
     tokens, width = h_hbm.shape
     half = length // 2
@@ -1695,7 +1705,9 @@
     sub = own_ref.shape[1]
     cuts = PIECE // sub
     early = number * 6 * cuts
-    line = LineSum(early + 2 * cuts, own_ref, other_ref, inbox, across, mine, (line_send, line_recv, mid_send, mid_recv, side_send, side_recv, line_store, line_load))
+    line = LineSum(own_ref.shape[0], own_ref, other_ref, inbox, across, mine, (line_send, line_recv, mid_send, mid_recv, side_send, side_recv, line_store, line_load))
+
+    small_line = LineSum(1, own_rest_ref, other_rest_ref, rest_inbox, rest_across, rest_mine, [rest_sems.at[k] for k in range(8)])
 
     def source(t):
         return pieces_ref.at[t // cuts, pl.ds(pl.multiple_of(lax.rem(t, cuts) * sub, sub), sub)]
@@ -1918,7 +1930,7 @@
             tick(at_tick[0])
             at_tick[0] += 1
 
-    def backward(packs, table, keys, values, keys_t, grad_q, grad_k, grad_v, acc, full_buf, ga, pack_out, wbuf, total, grad_middle, dgain, col, small, columns, cot, wo, attn, x_in, h_attn, h_ref, middle_ref, wr_ref, gains_ref, lse_ref):
+    def backward(packs, table, keys, values, keys_t, grad_q, grad_k, grad_v, acc, full_buf, ga, pack_out, wbuf, total, grad_middle, dgain, dwr, col, small, columns, cot, wo, attn, x_in, h_attn, h_ref, middle_ref, wr_ref, gains_ref, lse_ref):
         ws = GroupSum(small, small.shape[1], lands, None, sems(2), None, free, False, core, group)
         cs = GroupSum(columns, PIECE + 16, lands, None, sems(3), None, free, False, core, group)
         copies = [
@@ -1942,9 +1954,6 @@
         ]
         for copy in copies:
             copy.start()
-        small[:, 256:384, :] = jnp.zeros((8, 128, PIECE), BF16)
-        late_pieces[384:PIECE, :] = jnp.zeros((PIECE - 384, PIECE), BF16)
-        columns[:, PIECE:, :] = jnp.zeros((8, 16, PIECE), BF16)
         go_on(2)
         gx.over_x(go_on)
         go_on(2)
@@ -1978,13 +1987,12 @@
         ga_exchange = (ga, ga_in, ga_send, ga_recv, local_sems.at[2], n)
         exchange_start(*ga_exchange)
         go_on()
-        col[:, :128] = dot(h, grad_logits, TN).astype(BF16)
+        dwr[...] = dot(grad_logits, h, TN)[:EXPERTS]
         for r in range(8):
             at = strip(r)
             dwo = dot(attn[at], grad_branch, TN).astype(BF16)
             small[r, 0:128, :] = dwo[:, :PIECE]
             small[r, 128:256, :] = dwo[:, PIECE:]
-            small[r, 256:384, 0:128] = col[pl.ds(pl.multiple_of(at * 128, 128), 128), 0:128]
         ws.start()
         ys.start()
         go_on()
@@ -2095,7 +2103,7 @@
         ys.over_x()
         go_on(2)
         total[...] = jnp.zeros_like(total)
-        late_pieces[:384] = ws.finish().astype(BF16)
+        late_pieces[:256] = ws.finish().astype(BF16)
         ws.release()
         ffn = ys.finish()
         mixed_ref[...] = middle_ref[...] + RESIDUAL * jnp.concatenate([ffn[:tokens], ffn[tokens:]], 1)
@@ -2137,9 +2145,11 @@
         grad_x_ref[...] = grad_middle[...] + norm_back(grad_h * gains_ref[0:1], normed, scale)
         for r in range(8):
             at = pl.ds(pl.multiple_of(strip(r) * 128, 128), 128)
-            row = row_iota((16, 128))
-            both = jnp.where(row == 0, dgain[0:1, at], jnp.where(row == 1, dgain[1:2, at], 0.0))
-            columns[r, PIECE:, 0:128] = both.astype(BF16)
+            router_rows = jnp.concatenate([dwr[q * 8 : (q + 1) * 8, at] for q in range(EXPERTS // 8)], 1)
+            row = row_iota((8, 128))
+            gain_rows = jnp.where(row == 0, dgain[0:1, at], jnp.where(row == 1, dgain[1:2, at], 0.0))
+            gain_rows = jnp.concatenate([gain_rows, jnp.zeros((8, PIECE - 128), F32)], 1)
+            columns[r, PIECE:, :] = jnp.concatenate([router_rows, gain_rows], 0).astype(BF16)
         cs.start()
         go_on()
         cs.over_cores()
@@ -2147,8 +2157,8 @@
         cs.over_x(go_on)
         go_on(3)
         summed = cs.finish().astype(BF16)
-        late_pieces[PIECE:] = summed[:PIECE]
-        late_pieces[384:400] = summed[PIECE:]
+        late_pieces[256:] = summed[:PIECE]
+        late_rest[...] = summed[PIECE:]
 
     f32, bf = (lambda *shape: pltpu.VMEM(shape, F32)), (lambda *shape: pltpu.VMEM(shape, BF16))
     pl.run_scoped(
@@ -2169,8 +2179,9 @@
         f32(tokens, width),
         f32(tokens, width),
         f32(8, width),
+        f32(EXPERTS, width),
         bf(width, PACK),
-        bf(8, 384, PIECE),
+        bf(8, 256, PIECE),
         bf(8, PIECE + 16, PIECE),
         f32(tokens, width),
         bf(*wo_hbm.shape),
@@ -2197,8 +2208,12 @@
         line.tick(t, late_source)
         return carry
 
-    lax.fori_loop(early, line.count + LAG_END, late, 0)
+    for t in range(1 + LAG_END):
+        small_line.tick(jnp.int32(t), lambda t: late_rest)
+        late(jnp.int32(early + t), 0)
+    lax.fori_loop(early + 1 + LAG_END, line.count + LAG_END, late, 0)
     line.finish()
+    small_line.finish()
 
 
 def backward_step(ends, xs, gs, gates, w_gate, w_up, w_down, cxs, rest, diag, full, weights, packs, table, cot, wo, attn, x, h_attn, h, middle, wr, gains, lse, n, length, capp):
@@ -2210,15 +2225,18 @@
     shaped = lambda shape, dtype=BF16: jax.ShapeDtypeStruct(shape, dtype)
     sub = PIECE // 2
     piece = (sub, PIECE)
-    count = (number * 6 + 2) * 2
+    count = number * 12 + 3
+    rest_shape = (16, PIECE)
     land_rows = max(2 * (tokens + EXPERTS), PIECE + 16)
     return pl.pallas_call(
         functools.partial(backward_kernel, n, length, capp),
         in_specs=[smem] + [hbm] * 23,
-        out_specs=[hbm] * 7 + [vmem, vmem],
+        out_specs=[hbm] * 9 + [vmem, vmem],
         out_shape=[
             shaped((count,) + piece),
             shaped((count,) + piece),
+            shaped((1,) + rest_shape),
+            shaped((1,) + rest_shape),
             shaped((number * 6, PIECE, PIECE)),
             shaped(xs.shape),
             shaped(xs.shape),
@@ -2238,7 +2256,11 @@
             pltpu.VMEM((2, 2 * tokens, PIECE), BF16),
             pltpu.VMEM((2 * tokens, PIECE), BF16),
             pltpu.VMEM((2, 2 * tokens, PIECE), BF16),
-            pltpu.VMEM((2 * PIECE, PIECE), BF16),
+            pltpu.VMEM((768, PIECE), BF16),
+            pltpu.VMEM(rest_shape, BF16),
+            pltpu.VMEM((RING,) + rest_shape, BF16),
+            pltpu.VMEM((RING,) + rest_shape, BF16),
+            pltpu.VMEM((4,) + rest_shape, BF16),
             pltpu.VMEM((n, tokens, 128), BF16),
             pltpu.VMEM((n, tokens, PACK), BF16),
             dma(RING),
@@ -2263,6 +2285,7 @@
             dma(4),
             dma(2, 2),
             dma(2, 8),
+            dma(8, RING),
         ],
         compiler_params=params(63, collective_id=0, has_side_effects=True),
         cost_estimate=cost(6e10, 1e9),
@@ -2335,7 +2358,7 @@
         wo, wr = wo.reshape(n, 128, width), wr.reshape(width, 128)
         packs = packs.reshape(n, 2, rows, PACK)
         lse, full, middle, h_ffn, attn, xs, gs, gates, cx_rest, diag = attend(ends, packs, cxs, wo, wr, x, gains, length, number, capp)
-        own, other, _, _, _, _, _, grad_x, mixed = backward_step(
+        own, other, own_rest, other_rest, _, _, _, _, _, grad_x, mixed = backward_step(
             ends,
             merge(xs),
             merge(gs),
@@ -2364,9 +2387,8 @@
             length,
             capp,
         )
-        own, other = own.reshape(-1, PIECE, PIECE), other.reshape(-1, PIECE, PIECE)
         shapes = [w.shape for w in (w_gate, w_up, w_down)]
-        outs = tail(index, own, other, mixed, grad_x, shapes, shard)
+        outs = tail(index, own, other, own_rest, other_rest, mixed, grad_x, shapes, shard)
         return (
             outs[3].reshape(inputs.shape),
             outs[4].reshape(inputs.shape),
@@ -2418,7 +2440,7 @@
     grads = lax.all_to_all(grads.reshape(n, tokens, PACK), "ctx", split_axis=0, concat_axis=0, tiled=True)
     dw, grad_x, dgain_one = final_step(grads, weights, h_attn, x, gain_one, grad_middle, shard)
     mixed = middle + RESIDUAL * group_reduce(y_part, bits).astype(F32)
-    own = line_sum(pieces, n)
+    own = line_sum(pieces.reshape(-1, PIECE // 2, PIECE), n)
     other = swap(own, "ctx", 1)
     scatter = lambda a: lax.psum(lax.psum_scatter(a, "fsdp", scatter_dimension=0, tiled=True), "ctx").astype(F32)
     dwo = scatter(dwo)[:, :head_lanes, :].reshape(shard, width)

time: 550 us -> 543 us (0.987)
  Pallas kernels: 538 us -> 531 us
    pallas_call x1, Pallas kernels: 392 us -> 385 us  [backward_step(): pl.pallas_call(functools.partial(backward_kernel, n, length, capp), in_sp...]
where the time goes in v3:
time: 543 us; the launch traced here: 534 us
  Pallas kernels  531 us (98%)
    pallas_call x1, Pallas kernels, backward_step(): pl.pallas_call(functools.partial(backward_kernel, n, length, capp), in_sp...  385 us
    pallas_call x1, Pallas kernels, attend(): pl.pallas_call(functools.partial(attend_kernel, length, n, number, capp),...  60.7 us
    pallas_call x1, Pallas kernels, front(): pl.pallas_call(functools.partial(front_kernel, n, cap), in_specs=[vmem, v...  56.5 us
    pallas_call x1, Pallas kernels, tail(): pl.pallas_call(functools.partial(tail_kernel, number), grid_spec=pltpu.Pr...  28.5 us

profile of v3, /device:TPU:0, one launch (start us, length us, event | category | flops | bytes accessed | tf_op | source)
XLA Modules:
  0.0 534.2 jit_solution(5604796455833197917)
XLA Ops:
  0.6 0.7 stack.21
  1.3 0.7 stack.22
  2.0 0.6 pad_maximum_fusion.gain_ref
  2.5 56.5 %front.1 = (bf16[8,256,256]{2,1,0:T(8,128)(2,1)}, bf16[256,1024]{1,0:T(8,128)(2,1)}, bf16[2,4,288,1024]{3,2,1,0:T(8,128)(2,1)}, bf16[4,2,128,1024]{3,2,1,0:T(8,1...) custom-call(bf16[256,1024]{1,0:T(8,128)(2,1)} %wq_ref.1, ...), custom_call_target="tpu_custom_call" | custom-call | flops 2000000000 | bytes 50000000 | tf_op jit(solution)/shard_map/front/pallas_call | solution.py:1047
  59.0 60.7 %attend.1 = (f32[8,1,512]{2,1,0:T(1,128)}, f32[8,128,512]{2,1,0:T(8,128)}, f32[256,1024]{1,0:T(8,128)}, bf16[256,1024]{1,0:T(8,128)(2,1)}, bf16[8,256,128]{2,1,0...) custom-call(s32[1,4]{1,0:T(1,128)} %ends_ref.3, ...), custom_call_target="tpu_custom_call" | custom-call | flops 20000000000 | bytes 70000000 | tf_op jit(solution)/shard_map/attend/pallas_call | solution.py:1333
  119.7 384.9 %backward_step.1 = (bf16[51,256,512]{2,1,0:T(8,128)(2,1)}, bf16[51,256,512]{2,1,0:T(8,128)(2,1)}, bf16[1,16,512]{2,1,0:T(8,128)(2,1)}, bf16[1,16,512]{2,1,0:T(8,...) custom-call(s32[1,4]{1,0:T(1,128)} %ends_ref.3, ...), custom_call_target="tpu_custom_call" | custom-call | flops 60000002048 | bytes 1000000000 | tf_op jit(solution)/shard_map/backward_step/pallas_call | solution.py:2231
  504.6 0.7 pad_add_fusion.index_ref
  505.3 28.5 %tail.1 = (f32[8,1024,512]{2,1,0:T(8,128)}, f32[8,1024,512]{2,1,0:T(8,128)}, f32[8,512,1024]{2,1,0:T(8,128)}, f32[256,1024]{1,0:T(8,128)}, f32[256,1024]{1,0:T(8...) custom-call(s32[2]{0:T(128)} %pad_add_fusion.index_ref, ...), custom_call_target="tpu_custom_call" | custom-call | bytes 100000000 | tf_op jit(solution)/shard_map/tail/pallas_call | solution.py:766

commit v4 on v3

--- a/solution.py
+++ b/solution.py
@@ -1200,17 +1200,42 @@
         to_core(2).start()
         cx_cross().start()
 
+    halves = [pl.ds(k * split, split) for k in range(2)]
+
+    def hop(i, k):
+        return send(hs.at[0, halves[k]], hs.at[(1, 2, 4)[i], halves[k]], hop_send.at[i, k], hop_recv.at[i, k], (group[0], group[1], core)[i])
+
+    def form(k):
+        own_rows(k).wait()
+        for d in range(1, n):
+            from_device(lax.rem(ctx + d, n), k).wait_recv()
+        at = slice(k * split, (k + 1) * split)
+        total = None
+        for c in range(n):
+            part = dot(arrived[c, at, :], wo_ref[c])
+            total = part if total is None else total + part
+        middle = x_ref[at, :] + RESIDUAL * total
+        middle_ref[at, :] = middle
+        normed, _ = norm_parts(middle)
+        h = (normed * gain_ref[1:2]).astype(BF16)
+        h_ref[at, :] = h
+        hs[0, at, :] = h
+        for i in range(3):
+            hop(i, k).start()
+
+    @pl.when(block == per_half + 1)
+    def _():
+        for copy in copies:
+            copy.wait()
+        form(0)
+
     @pl.when(block == last)
     def _():
         order = (0, 4, 1, 2, 3, 5, 6, 7)
-        halves = [pl.ds(k * split, split) for k in range(2)]
 
         def load(step):
             refs = (cxs_ref.at[0], cxs_ref.at[1], rest_ref.at[0], diag_ref.at[0], rest_ref.at[1], rest_ref.at[2], rest_ref.at[3], diag_ref.at[1])
             return pltpu.make_async_copy(refs[order[step]], cx.at[step % 2], load_sems.at[step % 2])
-
-        def hop(i, k):
-            return send(hs.at[0, halves[k]], hs.at[(1, 2, 4)[i], halves[k]], hop_send.at[i, k], hop_recv.at[i, k], (group[0], group[1], core)[i])
 
         def cross(i):
             return send(hs.at[1 + i, halves[i]], hs.at[3, halves[i]], cross_send.at[i], cross_recv.at[i], group[1 - i])
@@ -1222,25 +1247,9 @@
         for i in range(3):
             to_core(i).wait_recv()
         load(1).start()
-        for copy in copies:
-            copy.wait()
-        for k in range(2):
-            own_rows(k).wait()
-            for d in range(1, n):
-                from_device(lax.rem(ctx + d, n), k).wait_recv()
-            at = slice(k * split, (k + 1) * split)
-            total = None
-            for c in range(n):
-                part = dot(arrived[c, at, :], wo_ref[c])
-                total = part if total is None else total + part
-            middle = x_ref[at, :] + RESIDUAL * total
-            middle_ref[at, :] = middle
-            normed, _ = norm_parts(middle)
-            h = (normed * gain_ref[1:2]).astype(BF16)
-            h_ref[at, :] = h
-            hs[0, at, :] = h
-            for i in range(3):
-                hop(i, k).start()
+        hop(0, 0).wait_recv()
+        cross(0).start()
+        form(1)
         keep = pltpu.make_async_copy(arrived, kept_ref, local_sems.at[2])
         keep.start()
 
@@ -1284,8 +1293,6 @@
         for k in range(2):
             hop(2, k).wait_recv()
         place(1)
-        hop(0, 0).wait_recv()
-        cross(0).start()
         hop(1, 0).wait_recv()
         hop(1, 1).wait_recv()
         cross(1).start()

time: 543 us -> 543 us (level)
  no operation moved by 1% of the time
where the time goes in v4:
time: 543 us; the launch traced here: 534 us
  Pallas kernels  531 us (98%)
    pallas_call x1, Pallas kernels, backward_step(): pl.pallas_call(functools.partial(backward_kernel, n, length, capp), in_sp...  384 us
    pallas_call x1, Pallas kernels, attend(): pl.pallas_call(functools.partial(attend_kernel, length, n, number, capp),...  62 us
    pallas_call x1, Pallas kernels, front(): pl.pallas_call(functools.partial(front_kernel, n, cap), in_specs=[vmem, v...  56.5 us
    pallas_call x1, Pallas kernels, tail(): pl.pallas_call(functools.partial(tail_kernel, number), grid_spec=pltpu.Pr...  28.5 us

profile of v4, /device:TPU:0, one launch (start us, length us, event | category | flops | bytes accessed | tf_op | source)
XLA Modules:
  0.0 534.4 jit_solution(8577792348036353713)
XLA Ops:
  0.6 0.7 stack.21
  1.3 0.7 stack.22
  2.0 0.6 pad_maximum_fusion.gain_ref
  2.5 56.5 %front.1 = (bf16[8,256,256]{2,1,0:T(8,128)(2,1)}, bf16[256,1024]{1,0:T(8,128)(2,1)}, bf16[2,4,288,1024]{3,2,1,0:T(8,128)(2,1)}, bf16[4,2,128,1024]{3,2,1,0:T(8,1...) custom-call(bf16[256,1024]{1,0:T(8,128)(2,1)} %wq_ref.1, ...), custom_call_target="tpu_custom_call" | custom-call | flops 2000000000 | bytes 50000000 | tf_op jit(solution)/shard_map/front/pallas_call | solution.py:1047
  59.0 62.0 %attend.1 = (f32[8,1,512]{2,1,0:T(1,128)}, f32[8,128,512]{2,1,0:T(8,128)}, f32[256,1024]{1,0:T(8,128)}, bf16[256,1024]{1,0:T(8,128)(2,1)}, bf16[8,256,128]{2,1,0...) custom-call(s32[1,4]{1,0:T(1,128)} %ends_ref.3, ...), custom_call_target="tpu_custom_call" | custom-call | flops 20000000000 | bytes 70000000 | tf_op jit(solution)/shard_map/attend/pallas_call | solution.py:1340
  121.0 383.8 %backward_step.1 = (bf16[51,256,512]{2,1,0:T(8,128)(2,1)}, bf16[51,256,512]{2,1,0:T(8,128)(2,1)}, bf16[1,16,512]{2,1,0:T(8,128)(2,1)}, bf16[1,16,512]{2,1,0:T(8,...) custom-call(s32[1,4]{1,0:T(1,128)} %ends_ref.3, ...), custom_call_target="tpu_custom_call" | custom-call | flops 60000002048 | bytes 1000000000 | tf_op jit(solution)/shard_map/backward_step/pallas_call | solution.py:2238
  504.8 0.7 pad_add_fusion.index_ref
  505.5 28.5 %tail.1 = (f32[8,1024,512]{2,1,0:T(8,128)}, f32[8,1024,512]{2,1,0:T(8,128)}, f32[8,512,1024]{2,1,0:T(8,128)}, f32[256,1024]{1,0:T(8,128)}, f32[256,1024]{1,0:T(8...) custom-call(s32[2]{0:T(128)} %pad_add_fusion.index_ref, ...), custom_call_target="tpu_custom_call" | custom-call | bytes 100000000 | tf_op jit(solution)/shard_map/tail/pallas_call | solution.py:766
